TPU v7x, 32 devices: a whole 2x2x4 slice. The times are simulated.
32 devices in a mesh: groups: 2 (over y), gx: 4 (over z), gy: 2 (over x), gz: 2 (over core).
Axes of the slice: x: 2, y: 2, z: 4, core: 2. Of those that a mesh axis runs over, the one named last changes fastest.
Arguments:
- positions: float32 [3, 8, 2, 2, 128], P(None, ('groups', 'gx'), 'gy', 'gz'), parts along dimension 1, may hold values from 0 to 1
- species: int32 [8, 2, 2, 128], P(('groups', 'gx'), 'gy', 'gz'), parts along dimension 0, may hold values from 0 to 4
- neighbours: int32 [8, 2, 2, 16, 128], P(('groups', 'gx'), 'gy', 'gz'), parts along dimension 0, may hold values from -1 to 559, as said below
- send_list: int32 [8, 2, 2, 16], P(('groups', 'gx'), 'gy', 'gz'), parts along dimension 0, may hold values from 0 to 127, as said below
- embedding: float32 [5, 128], replicated, may hold values from -6 to 6
- radial_in: float32 [8, 64], replicated, may hold values from -3 to 3
- radial_out_one: float32 [64, 256], replicated, may hold values from -0.1875 to 0.1875
- radial_in_two: float32 [8, 64], replicated, may hold values from -3 to 3
- radial_out_two: float32 [64, 512], replicated, may hold values from -0.1875 to 0.1875
- mix_scalar_one: float32 [128, 128], replicated, may hold values from -0.5 to 0.5
- mix_square_one: float32 [128, 128], replicated, may hold values from -0.25 to 0.25
- mix_vector_one: float32 [128, 128], replicated, may hold values from -0.5 to 0.5
- mix_scalar_two: float32 [128, 128], replicated, may hold values from -0.5 to 0.5
- mix_square_two: float32 [128, 128], replicated, may hold values from -0.1875 to 0.1875
- readout: float32 [128], replicated, may hold values from -1 to 1
Outputs:
- forces: float32 [3, 8, 2, 2, 128], P(None, ('groups', 'gx'), 'gy', 'gz'), parts along dimension 1
- atom_energy: float32 [8, 2, 2, 128], P(('groups', 'gx'), 'gy', 'gz'), parts along dimension 0
There are 2 independent parts, one for each index of `groups`. A program takes and returns all parts, laid end to end along the dimension named above; an argument that names none is the same for every part. Nothing has to cross between parts.
Inputs may be any that keep to these rules, and one draw needn't show every extreme that they name: `neighbours`: each entry is -1 (an empty slot) or an index into the extended list of 560 atoms; it never names the atom itself nor block 13; empty slots of an atom come after its used ones; an atom has at least 8 used slots, and in every domain some atom uses all 16. `send_list`: 16 distinct atoms of the domain.
All inputs are finite; a program needn't handle non-finite values.
Results may differ from a plain program's by a relative error of at most 0.0003.
Values sent between devices are 32-bit elements; how exact they have to be, the bound alone decides.
No kernel may reach another device: no remote copies, remote signals or barrier semaphores. Data moves between devices by JAX's collectives and lax.ppermute only.
A program may use at most 128 MiB of HBM per device.

v0:
```python
import functools
import itertools

import jax
import jax.numpy as jnp
from jax import lax
from jax.experimental import pallas as pl
from jax.experimental.pallas import tpu as pltpu
from jax.sharding import PartitionSpec as P

MESSAGE_SCALE = 0.125
CUTOFF_SQUARED = 16.0
AXES = ("gx", "gy", "gz")
LANES = 128
GHOSTS = 16
REACH = 5
VMEM_BYTES = 52 * 1024 * 1024
F32 = jnp.float32
BF16 = jnp.bfloat16


def window_size(count):
    return min(count, REACH)


def window_place(relative, base, count):
    if count > REACH:
        return relative + 2
    place = relative + base
    for _ in range(2):
        place = jnp.where(place < 0, place + count, place)
    for _ in range(2):
        place = jnp.where(place >= count, place - count, place)
    return place


def near_steps(count):
    return [0, 1, -1][: min(count, 3)]


def near_place(step, count):
    if count >= 3:
        return jnp.where(step < 0, step + 3, step)
    return jnp.where(step == 0, 0, 1)


def split(x):
    high = x.astype(BF16)
    return high, (x - high.astype(F32)).astype(BF16)


def split_wide(x):
    high = x.astype(BF16).astype(F32)
    return high, x - high


def weight_stack(w):
    high, low = split(w)
    return jnp.concatenate([high, low, high], axis=0)


def data_stack(x):
    high, low = split(x)
    return jnp.concatenate([high, high, low], axis=0)


def dot_nn(a, b):
    return lax.dot_general(a, b, (((1,), (0,)), ((), ())), preferred_element_type=F32)


def dot_tn(a, b):
    return lax.dot_general(a, b, (((0,), (0,)), ((), ())), preferred_element_type=F32)


def dot_nt(a, b):
    return lax.dot_general(a, b, (((1,), (1,)), ((), ())), preferred_element_type=F32)


def product_nn(w_high, w_low, x):
    high, low = split(x)
    return dot_nn(w_high, high) + dot_nn(w_low, high) + dot_nn(w_high, low)


def sigmoid(v):
    return 1.0 / (1.0 + jnp.exp(-v))


def pick_lanes(row, index):
    return jnp.take_along_axis(jnp.broadcast_to(row, index.shape), index, axis=1)


def iota(shape, dim):
    return lax.broadcasted_iota(jnp.int32, shape, dim)


def pack_kernel(copies, send_ref, pos_ref, species_ref, neigh_ref, out_ref):
    lane = iota((8, LANES), 1)
    row = iota((8, LANES), 0)
    sent = jnp.zeros((8, LANES), jnp.int32)
    for s in range(GHOSTS):
        sent = jnp.where((lane & (GHOSTS - 1)) == s, send_ref[0, 0, 0, s], sent)
    block = jnp.zeros((8, LANES), F32)
    for x in range(3):
        block = jnp.where(row == x, pos_ref[x, 0, 0], block)
    block = jnp.where(row == 3, species_ref[0, 0].astype(F32), block)
    neigh = neigh_ref[0, 0, 0]
    for half in range(2):
        lists = jnp.take_along_axis(neigh[half * 8 : half * 8 + 8], sent, axis=1).astype(F32)
        kept = jnp.where((lane >> 4) == row, lists, 0.0)
        block = jnp.where(row == 4 + half, jnp.sum(kept, axis=0, keepdims=True), block)
    block = jnp.where(row == 6, sent.astype(F32), block)
    for w in range(copies):
        out_ref[w] = block


def forces_kernel(count, send_ref, parts_ref, out_ref):
    total = parts_ref[0]
    for w in range(1, count):
        total = total + parts_ref[w]
    lane = iota((8, LANES), 1)
    slot = jnp.full((8, LANES), -1, jnp.int32)
    for s in range(GHOSTS):
        slot = jnp.where(lane == send_ref[0, 0, 0, s], s, slot)
    moved = jnp.take_along_axis(total, jnp.maximum(slot, 0), axis=1)
    moved = jnp.where(slot >= 0, moved, 0.0)
    for x in range(3):
        out_ref[x, 0, 0] = -(total[x : x + 1] + moved[4 + x : 5 + x])


def main_kernel(
    dims,
    near,
    base_ref,
    table_ref,
    neigh_ref,
    embedding_ref,
    win_one_ref,
    wout_one_ref,
    win_two_ref,
    wout_two_ref,
    mss_one_ref,
    msq_one_ref,
    mv_one_ref,
    mss_two_ref,
    msq_two_ref,
    readout_ref,
    grad_ref,
    energy_ref,
    r_ref,
    kind_ref,
    dist_ref,
    wh_ref,
    slope_ref,
    wh2_ref,
    slope2_ref,
    moment_ref,
    pair_ref,
    target_ref,
    feat_ref,
    source_ref,
    radial_ref,
    node_ref,
    dsource_ref,
    dradial_ref,
    dr_ref,
    dmoment_ref,
):
    nx, ny, nz = dims
    wsize = tuple(window_size(n) for n in dims)
    windows = wsize[0] * wsize[1] * wsize[2]
    halves = -(-windows * GHOSTS // LANES)
    groups = 1 + -(-len(near) // 8)
    channels = LANES
    kinds = embedding_ref.shape[0]
    hidden = win_one_ref.shape[1]
    basis = win_one_ref.shape[0]
    own_edges = 16 * LANES
    atoms = groups * LANES

    lane16 = iota((16, LANES), 1)
    sub16 = iota((16, LANES), 0)
    lane8 = iota((8, LANES), 1)
    sub8 = iota((8, LANES), 0)
    bases = [base_ref[a] for a in range(3)]
    near_sizes = [len(near_steps(n)) for n in dims]

    def flat(steps):
        places = [window_place(steps[a], bases[a], dims[a]) for a in range(3)]
        return (places[0] * wsize[1] + places[1]) * wsize[2] + places[2]

    own_place = flat((0, 0, 0))
    near_places = [flat(step) for step in near]

    sent = [jnp.zeros((8, LANES), F32) for _ in range(halves)]
    for w in range(windows):
        block = table_ref[w]
        index = jnp.broadcast_to(block[6:7], (8, LANES)).astype(jnp.int32)
        picked = jnp.take_along_axis(block, index, axis=1)
        sent[w // 8] = jnp.where((lane8 >> 4) == w % 8, picked, sent[w // 8])

    for g in range(groups):
        members = [] if g == 0 else list(range((g - 1) * 8, min(g * 8, len(near))))
        if g == 0:
            entries = neigh_ref[0, 0, 0]
            own_block = table_ref[own_place]
            centre = [own_block[x : x + 1] for x in range(3)]
            steps = [0, 0, 0]
        else:
            centre8 = jnp.zeros((8, LANES), F32)
            listed = [jnp.full((8, LANES), -1.0, F32) for _ in range(2)]
            steps = [jnp.zeros((16, LANES), jnp.int32) for _ in range(3)]
            for q in members:
                block = table_ref[near_places[q]]
                here = (lane8 >> 4) == q % 8
                index = jnp.broadcast_to(block[6:7], (8, LANES)).astype(jnp.int32)
                centre8 = jnp.where(here, jnp.take_along_axis(block, index, axis=1), centre8)
                for half in range(2):
                    rows = pick_lanes(block[4 + half : 5 + half], sub8 * 16 + (lane8 & 15))
                    listed[half] = jnp.where(here, rows, listed[half])
                for a in range(3):
                    if near[q][a]:
                        steps[a] = jnp.where((lane16 >> 4) == q % 8, near[q][a], steps[a])
            entries = jnp.concatenate(listed, axis=0).astype(jnp.int32)
            centre = [centre8[x : x + 1] for x in range(3)]
        valid = entries >= 0
        named = jnp.maximum(entries, 0)
        local = named < LANES
        local_index = jnp.where(local, named, 0)
        ghost = jnp.maximum(named - LANES, 0)
        block_id, slot = ghost >> 4, ghost & 15
        first = (block_id * 57) >> 9
        rest = block_id - first * 9
        second = (rest * 11) >> 5
        shift = [first - 1, second - 1, rest - second * 3 - 1]
        sent_index = flat([shift[a] + steps[a] for a in range(3)]) * GHOSTS + slot
        values = []
        for x in range(4):
            if g == 0:
                inside = pick_lanes(own_block[x : x + 1], local_index)
            else:
                inside = jnp.zeros((16, LANES), F32)
                for q in members:
                    rows = pick_lanes(table_ref[near_places[q], x : x + 1, :], local_index)
                    inside = jnp.where((lane16 >> 4) == q % 8, rows, inside)
            outside = jnp.zeros((16, LANES), F32)
            for h in range(halves):
                rows = pick_lanes(sent[h][x : x + 1], sent_index & (LANES - 1))
                outside = jnp.where((sent_index >> 7) == h, rows, outside)
            if x < 3:
                outside = outside + shift[x].astype(F32)
            values.append(jnp.where(local, inside, outside))
        relative = [values[x] - centre[x] for x in range(3)]
        square = relative[0] * relative[0] + relative[1] * relative[1] + relative[2] * relative[2]
        linear = 1.0 - square / CUTOFF_SQUARED
        scale = jnp.where(valid, MESSAGE_SCALE, 0.0)
        dist_ref[0, g * 16 : g * 16 + 16, :] = square
        dist_ref[1, g * 16 : g * 16 + 16, :] = linear * linear * scale
        dist_ref[2, g * 16 : g * 16 + 16, :] = linear * scale * (-2.0 / CUTOFF_SQUARED)
        for n in range(16):
            for x in range(3):
                r_ref[x, g * 16 + n] = jnp.broadcast_to(relative[x][n : n + 1], (8, LANES))
            kind_ref[g * 16 + n] = jnp.broadcast_to(values[3][n : n + 1], (8, LANES))
        if g == 0:
            steps_near = [near_place(shift[a], dims[a]) for a in range(3)]
            order = (steps_near[0] * near_sizes[1] + steps_near[1]) * near_sizes[2] + steps_near[2]
            row = jnp.where(local, local_index, LANES + (order - 1) * GHOSTS + slot)
            size = atoms
        else:
            row = jnp.where(local, local_index, LANES + sent_index)
            size = LANES + halves * LANES
        row = jnp.where(valid, row, -1)
        position = iota((size, LANES), 0)
        for n in range(16):
            hot = jnp.where(position == row[n : n + 1], 1.0, 0.0).astype(BF16)
            if g == 0:
                pair_ref[0:size, n * LANES : (n + 1) * LANES] = hot
                pair_ref[size : 2 * size, n * LANES : (n + 1) * LANES] = hot
            else:
                target_ref[g - 1, :, n * LANES : (n + 1) * LANES] = hot

    rates = jnp.zeros((basis, LANES), F32)
    basis_row = iota((basis, LANES), 0)
    for m in range(basis):
        rates = jnp.where(basis_row == m, 0.08 * 2.0 ** (m / 2.0), rates)

    def radial_weights(win_ref):
        win = win_ref[...]
        both = jnp.concatenate([win, -rates[:, :hidden] * win], axis=1)
        high, low = split_wide(both)
        return jnp.concatenate([high, high, low, low], axis=0).astype(BF16)

    def radial_rows(weights, octet):
        dist8 = dist_ref[0, pl.ds(octet * 8, 8), :]
        weight8 = dist_ref[1, pl.ds(octet * 8, 8), :]
        slope8 = dist_ref[2, pl.ds(octet * 8, 8), :]
        values = jnp.concatenate([jnp.exp(-rates * dist8[j : j + 1]) for j in range(8)], axis=1)
        high, low = split_wide(values)
        stacked = jnp.concatenate([high, low, high, low], axis=0).astype(BF16)
        both = dot_tn(weights, stacked)
        rows = []
        for j in range(8):
            before = both[:hidden, j * LANES : (j + 1) * LANES]
            change = both[hidden:, j * LANES : (j + 1) * LANES]
            gate = sigmoid(before)
            after = before * gate
            gain = gate * (1.0 + before * (1.0 - gate))
            weight = weight8[j : j + 1]
            rows.append((weight * after, slope8[j : j + 1] * after + weight * (gain * change)))
        return rows

    weights_one = radial_weights(win_one_ref)
    weights_two = radial_weights(win_two_ref)

    def radial_one_step(octet, carry):
        for j, (value, slope) in enumerate(radial_rows(weights_one, octet)):
            wh_ref[octet * 8 + j] = value
            slope_ref[octet * 8 + j] = slope
        return carry

    lax.fori_loop(0, groups * 2, radial_one_step, 0)

    def radial_two_step(octet, carry):
        rows = radial_rows(weights_two, octet)
        lanes = pl.ds(pl.multiple_of(octet * 8 * LANES, 8 * LANES), 8 * LANES)
        stack = data_stack(jnp.concatenate([value for value, _ in rows], axis=1))
        wh2_ref[:, lanes] = stack
        for j, (_, slope) in enumerate(rows):
            slope2_ref[octet * 8 + j] = slope
        return carry

    lax.fori_loop(0, 2, radial_two_step, 0)

    def moment_step(step, carry):
        g, part = step // (hidden // 8), step % (hidden // 8)
        rows = pl.ds(pl.multiple_of(part * 8, 8), 8)
        lanes = pl.ds(pl.multiple_of(g * LANES, LANES), LANES)
        sums = [[jnp.zeros((8, LANES), F32) for _ in range(4)] for _ in range(kinds)]
        for n in range(16):
            e = g * 16 + n
            value = wh_ref[e, rows, :]
            parts = [value] + [value * r_ref[x, e] for x in range(3)]
            kind = kind_ref[e]
            for s in range(kinds):
                mask = kind == float(s)
                for j in range(4):
                    sums[s][j] = sums[s][j] + jnp.where(mask, parts[j], 0.0)
        for s in range(kinds):
            for j in range(4):
                place = pl.ds(pl.multiple_of(s * hidden + part * 8, 8), 8)
                moment_ref[j, place, lanes] = sums[s][j]
        return carry

    lax.fori_loop(0, groups * (hidden // 8), moment_step, 0)

    wout_one = wout_one_ref[...]
    combined = []
    for j in range(2):
        columns = wout_one[:, j * channels : (j + 1) * channels]
        rows = [columns * embedding_ref[s : s + 1, :] for s in range(kinds)]
        combined.append(jnp.concatenate(rows, axis=0))
    stacked_weights = [weight_stack(w) for w in combined]
    scalar_one = dot_tn(stacked_weights[0], data_stack(moment_ref[0]))
    vector_one = [dot_tn(stacked_weights[1], data_stack(moment_ref[1 + x])) for x in range(3)]
    squares_one = sum(v * v for v in vector_one)
    mss_one, msq_one, mv_one = mss_one_ref[...], msq_one_ref[...], mv_one_ref[...]
    mix_one = jnp.concatenate([weight_stack(mss_one), weight_stack(msq_one)], axis=0)
    before_one = dot_tn(
        mix_one, jnp.concatenate([data_stack(scalar_one), data_stack(squares_one)], axis=0)
    )
    gate_one = sigmoid(before_one)
    mv_stack = weight_stack(mv_one)
    features = [before_one * gate_one] + [dot_tn(mv_stack, data_stack(v)) for v in vector_one]
    gain_one = gate_one * (1.0 + before_one * (1.0 - gate_one))
    for j in range(4):
        rows = slice(j * channels, (j + 1) * channels)
        feat_ref[rows, 0:atoms], feat_ref[rows, atoms : 2 * atoms] = split(features[j])
    node_ref[4, :, 0:atoms] = gain_one
    for x in range(3):
        node_ref[5 + x, :, 0:atoms] = vector_one[x]

    wout_two = wout_two_ref[...]
    wout_two_high, wout_two_low = split(wout_two)
    radial_stack = jnp.concatenate([wout_two_high, wout_two_low, wout_two_high], axis=0)

    def edge_step(step, carry):
        lanes = pl.ds(pl.multiple_of(step * 256, 256), 256)
        source_ref[:, lanes] = dot_nn(feat_ref[...], pair_ref[:, lanes])
        radial_ref[:, lanes] = dot_tn(radial_stack, wh2_ref[:, lanes])
        return carry

    lax.fori_loop(0, own_edges // 256, edge_step, 0)

    def sum_step(part, carry):
        def rows(j):
            return pl.ds(pl.multiple_of(j * channels + part * 8, 8), 8)

        sums = [jnp.zeros((8, LANES), F32) for _ in range(4)]
        for n in range(16):
            lanes = slice(n * LANES, (n + 1) * LANES)
            t = source_ref[rows(0), lanes]
            u = [source_ref[rows(1 + x), lanes] for x in range(3)]
            paths = [radial_ref[rows(j), lanes] for j in range(4)]
            r = [r_ref[x, n] for x in range(3)]
            along = r[0] * u[0] + r[1] * u[1] + r[2] * u[2]
            sums[0] = sums[0] + (paths[0] * t + paths[1] * along)
            turned = paths[2] * t
            for x in range(3):
                sums[1 + x] = sums[1 + x] + (turned * r[x] + paths[3] * u[x])
        for j in range(4):
            node_ref[j, pl.ds(pl.multiple_of(part * 8, 8), 8), 0:LANES] = sums[j]
        return carry

    lax.fori_loop(0, channels // 8, sum_step, 0)

    scalar_two = node_ref[0, :, 0:LANES]
    vector_two = [node_ref[1 + x, :, 0:LANES] for x in range(3)]
    squares_two = sum(v * v for v in vector_two)
    mss_two, msq_two = mss_two_ref[...], msq_two_ref[...]
    mix_two = jnp.concatenate([weight_stack(mss_two), weight_stack(msq_two)], axis=0)
    before_two = dot_tn(
        mix_two, jnp.concatenate([data_stack(scalar_two), data_stack(squares_two)], axis=0)
    )
    gate_two = sigmoid(before_two)
    readout = jnp.transpose(jnp.broadcast_to(readout_ref[...], (LANES, channels)))
    energy_ref[0, 0] = jnp.sum(readout * (before_two * gate_two), axis=0, keepdims=True)
    dbefore_two = readout * (gate_two * (1.0 + before_two * (1.0 - gate_two)))
    dscalar_two = product_nn(*split(mss_two), dbefore_two)
    dsquares_two = product_nn(*split(msq_two), dbefore_two)
    node_ref[0, :, 0:LANES] = dscalar_two
    for x in range(3):
        node_ref[1 + x, :, 0:LANES] = 2.0 * vector_two[x] * dsquares_two

    def back_step(n, carry):
        lanes = pl.ds(pl.multiple_of(n * LANES, LANES), LANES)
        r = [jnp.concatenate([r_ref[x, n]] * 2, axis=0) for x in range(3)]
        totals = [jnp.zeros((16, LANES), F32) for _ in range(3)]
        for part in range(channels // 16):

            def rows(j):
                return slice(j * channels + part * 16, j * channels + part * 16 + 16)

            t = source_ref[rows(0), lanes]
            u = [source_ref[rows(1 + x), lanes] for x in range(3)]
            paths = [radial_ref[rows(j), lanes] for j in range(4)]
            ds = node_ref[0, rows(0), 0:LANES]
            dv = [node_ref[1 + x, rows(0), 0:LANES] for x in range(3)]
            push = paths[1] * ds
            facing = r[0] * dv[0] + r[1] * dv[1] + r[2] * dv[2]
            along = r[0] * u[0] + r[1] * u[1] + r[2] * u[2]
            meeting = dv[0] * u[0] + dv[1] * u[1] + dv[2] * u[2]
            turned = paths[2] * t
            dsource = [paths[0] * ds + paths[2] * facing]
            for x in range(3):
                dsource.append(push * r[x] + paths[3] * dv[x])
                totals[x] = totals[x] + (push * u[x] + turned * dv[x])
            dradial = [ds * t, ds * along, t * facing, meeting]
            for j in range(4):
                dsource_ref[0, rows(j), lanes], dsource_ref[1, rows(j), lanes] = split(dsource[j])
                dradial_ref[0, rows(j), lanes], dradial_ref[1, rows(j), lanes] = split(dradial[j])
        for x in range(3):
            total = jnp.sum(totals[x], axis=0, keepdims=True)
            dr_ref[x : x + 1, lanes] = total
        return carry

    lax.fori_loop(0, 16, back_step, 0)

    dfeat = dot_nt(dsource_ref[0], pair_ref[0:atoms, :]) + dot_nt(
        dsource_ref[1], pair_ref[0:atoms, :]
    )

    def radial_back_step(step, carry):
        lanes = pl.ds(pl.multiple_of(step * 512, 512), 512)
        dhigh, dlow = dradial_ref[0, :, lanes], dradial_ref[1, :, lanes]
        dwh = dot_nn(wout_two_high, dhigh) + dot_nn(wout_two_low, dhigh) + dot_nn(wout_two_high, dlow)
        for j in range(4):
            n = step * 4 + j
            dd = jnp.sum(
                dwh[:, j * LANES : (j + 1) * LANES] * slope2_ref[n], axis=0, keepdims=True
            )
            at = pl.ds(pl.multiple_of(n * LANES, LANES), LANES)
            for x in range(3):
                dr_ref[x : x + 1, at] = dr_ref[x : x + 1, at] + 2.0 * dd * r_ref[x, n, 0:1, :]
        return carry

    lax.fori_loop(0, 4, radial_back_step, 0)

    gain_one = node_ref[4, :, 0:atoms]
    vector_one = [node_ref[5 + x, :, 0:atoms] for x in range(3)]
    dbefore_one = dfeat[0:channels] * gain_one
    dscalar_one = product_nn(*split(mss_one), dbefore_one)
    dsquares_one = product_nn(*split(msq_one), dbefore_one)
    mv_parts = split(mv_one)
    dmoment_ref[0] = product_nn(*split(combined[0]), dscalar_one)
    combined_parts = split(combined[1])
    for x in range(3):
        du = dfeat[(1 + x) * channels : (2 + x) * channels]
        dvector = 2.0 * vector_one[x] * dsquares_one + product_nn(*mv_parts, du)
        dmoment_ref[1 + x] = product_nn(*combined_parts, dvector)

    def one_back_step(step, carry):
        g = step // 4
        lanes = pl.ds(pl.multiple_of(g * LANES, LANES), LANES)
        edges = [step * 4 + j for j in range(4)]
        totals = [[jnp.zeros((8, LANES), F32) for _ in range(4)] for _ in range(4)]
        for part in range(hidden // 8):
            rows = slice(part * 8, part * 8 + 8)
            pulls = [
                [dmoment_ref[m, s * hidden + part * 8 : s * hidden + part * 8 + 8, lanes] for m in range(4)]
                for s in range(kinds)
            ]
            for j, e in enumerate(edges):
                kind = kind_ref[e]
                chosen = pulls[0]
                for s in range(1, kinds):
                    mask = kind == float(s)
                    chosen = [jnp.where(mask, pulls[s][m], chosen[m]) for m in range(4)]
                r = [r_ref[x, e] for x in range(3)]
                dwh = chosen[0] + r[0] * chosen[1] + r[1] * chosen[2] + r[2] * chosen[3]
                value = wh_ref[e, rows, :]
                totals[j][3] = totals[j][3] + dwh * slope_ref[e, rows, :]
                for x in range(3):
                    totals[j][x] = totals[j][x] + value * chosen[1 + x]
        for j, e in enumerate(edges):
            at = pl.ds(pl.multiple_of(e * LANES, LANES), LANES)
            dd = 2.0 * jnp.sum(totals[j][3], axis=0, keepdims=True)
            for x in range(3):
                change = jnp.sum(totals[j][x], axis=0, keepdims=True) + dd * r_ref[x, e, 0:1, :]
                dr_ref[4 + x : 5 + x, at] = change
        return carry

    lax.fori_loop(0, groups * 4, one_back_step, 0)

    pieces = []
    for e in range(groups * 16):
        at = slice(e * LANES, (e + 1) * LANES)
        piece = dr_ref[:, at]
        low = pltpu.roll(piece, 4, 0)
        if e < 16:
            piece = jnp.where((sub8 & 3) == 3, 0.0, piece + low)
        else:
            piece = jnp.where((sub8 & 3) == 3, 0.0, jnp.where(sub8 < 4, low, piece))
        pieces.append(piece)
    centres = [sum(pieces[g * 16 : g * 16 + 16]) for g in range(groups)]
    own_change = jnp.concatenate(pieces[:16], axis=1)
    own_high, own_low = split_wide(own_change)
    moved = dot_nt(jnp.concatenate([own_high, own_low], axis=0).astype(BF16), pair_ref[0:atoms, :])
    moved = moved[0:8] + moved[8:16]
    moved = [moved[:, g * LANES : (g + 1) * LANES] - centres[g] for g in range(groups)]

    sent_totals = [jnp.zeros((8, LANES), F32) for _ in range(halves)]
    inner = {}
    for g in range(1, groups):
        members = range((g - 1) * 8, min(g * 8, len(near)))
        change = jnp.concatenate(pieces[g * 16 : g * 16 + 16], axis=1)
        high, low = split_wide(change)
        owner = (iota(change.shape, 1) & (LANES - 1)) >> 4
        stack = [high, low]
        for q in members:
            here = owner == q % 8
            stack += [jnp.where(here, high, 0.0), jnp.where(here, low, 0.0)]
        spread = dot_nt(jnp.concatenate(stack, axis=0).astype(BF16), target_ref[g - 1])
        for h in range(halves):
            lanes = slice(LANES + h * LANES, 2 * LANES + h * LANES)
            sent_totals[h] = sent_totals[h] + (spread[0:8, lanes] + spread[8:16, lanes])
        for i, q in enumerate(members):
            at = 16 + i * 16
            inner[q] = spread[at : at + 8, 0:LANES] + spread[at + 8 : at + 16, 0:LANES]

    spot = lane8 & 15
    for w in range(windows):
        block = jnp.take_along_axis(sent_totals[w // 8], (w % 8) * 16 + spot, axis=1)
        grad_ref[w] = jnp.where(sub8 < 4, 0.0, block)
    grad_ref[own_place] = grad_ref[own_place] + jnp.where(sub8 < 4, moved[0], 0.0)
    for q in range(len(near)):
        block = jnp.take_along_axis(moved[1 + q // 8], (q % 8) * 16 + spot, axis=1)
        grad_ref[near_places[q]] = grad_ref[near_places[q]] + jnp.where(sub8 < 4, inner[q], block)


def send_along(value, axis, steps):
    count = lax.axis_size(axis)
    return lax.ppermute(value, axis, [(i, (i + steps) % count) for i in range(count)])


def axis_steps(count):
    return list(range(count)) if count <= REACH else list(range(-2, 3))


def per_device(
    positions,
    species,
    neighbours,
    send_list,
    embedding,
    radial_in,
    radial_out_one,
    radial_in_two,
    radial_out_two,
    mix_scalar_one,
    mix_square_one,
    mix_vector_one,
    mix_scalar_two,
    mix_square_two,
    readout,
):
    dims = tuple(lax.axis_size(axis) for axis in AXES)
    windows = 1
    for count in dims:
        windows *= window_size(count)
    whole = windows == dims[0] * dims[1] * dims[2] and windows <= 16
    near = [step for step in itertools.product(*[near_steps(n) for n in dims])][1:]
    groups = 1 + -(-len(near) // 8)
    halves = -(-windows * GHOSTS // LANES)
    atoms = groups * LANES
    hidden = radial_in.shape[1]
    kinds, channels = embedding.shape
    copies = windows if whole else 1
    smem = pl.BlockSpec(memory_space=pltpu.SMEM)
    vmem = pl.BlockSpec(memory_space=pltpu.VMEM)

    packed = pl.pallas_call(
        functools.partial(pack_kernel, copies),
        out_shape=jax.ShapeDtypeStruct((copies, 8, LANES), F32),
        in_specs=[smem, vmem, vmem, vmem],
        out_specs=vmem,
    )(send_list, positions, species, neighbours)

    if whole:
        table = lax.all_to_all(packed, AXES, 0, 0, tiled=True)
        base = jnp.stack([lax.axis_index(axis) for axis in AXES]).astype(jnp.int32)
    else:
        table = packed.reshape(1, 1, 1, 8, LANES)
        for dim, axis in reversed(list(enumerate(AXES))):
            parts = [
                send_along(table, axis, -step) if step else table for step in axis_steps(dims[dim])
            ]
            table = jnp.concatenate(parts, axis=dim)
        table = table.reshape(windows, 8, LANES)
        base = jnp.zeros((3,), jnp.int32)

    rows = groups * 16
    edges = 16 * LANES
    grads, energy = pl.pallas_call(
        functools.partial(main_kernel, dims, near),
        out_shape=(
            jax.ShapeDtypeStruct((windows, 8, LANES), F32),
            jax.ShapeDtypeStruct((1, 1, 1, LANES), F32),
        ),
        in_specs=[smem] + [vmem] * 13,
        out_specs=(vmem, vmem),
        scratch_shapes=[
            pltpu.VMEM((3, rows, 8, LANES), F32),
            pltpu.VMEM((rows, 8, LANES), F32),
            pltpu.VMEM((3, rows, LANES), F32),
            pltpu.VMEM((rows, hidden, LANES), F32),
            pltpu.VMEM((rows, hidden, LANES), F32),
            pltpu.VMEM((3 * hidden, edges), BF16),
            pltpu.VMEM((16, hidden, LANES), F32),
            pltpu.VMEM((4, kinds * hidden, atoms), F32),
            pltpu.VMEM((2 * atoms, edges), BF16),
            pltpu.VMEM((groups - 1, LANES + halves * LANES, edges), BF16),
            pltpu.VMEM((4 * channels, 2 * atoms), BF16),
            pltpu.VMEM((4 * channels, edges), F32),
            pltpu.VMEM((4 * channels, edges), F32),
            pltpu.VMEM((8, channels, atoms), F32),
            pltpu.VMEM((2, 4 * channels, edges), BF16),
            pltpu.VMEM((2, 4 * channels, edges), BF16),
            pltpu.VMEM((8, rows * LANES), F32),
            pltpu.VMEM((4, kinds * hidden, atoms), F32),
        ],
        compiler_params=pltpu.CompilerParams(vmem_limit_bytes=VMEM_BYTES),
    )(
        base,
        table,
        neighbours,
        embedding,
        radial_in,
        radial_out_one,
        radial_in_two,
        radial_out_two,
        mix_scalar_one,
        mix_square_one,
        mix_vector_one,
        mix_scalar_two,
        mix_square_two,
        readout.reshape(1, channels),
    )

    if whole:
        returned = lax.all_to_all(grads, AXES, 0, 0, tiled=True)
    else:
        returned = grads.reshape(tuple(window_size(n) for n in dims) + (8, LANES))
        for dim, axis in enumerate(AXES):
            total = None
            for place, step in enumerate(axis_steps(dims[dim])):
                part = lax.slice_in_dim(returned, place, place + 1, axis=dim)
                part = send_along(part, axis, step) if step else part
                total = part if total is None else total + part
            returned = total
        returned = returned.reshape(1, 8, LANES)

    forces = pl.pallas_call(
        functools.partial(forces_kernel, copies),
        out_shape=jax.ShapeDtypeStruct((3, 1, 1, 1, LANES), F32),
        in_specs=[smem, vmem],
        out_specs=vmem,
    )(send_list, returned)
    return (forces.reshape(3, 1, 1, 1, LANES), energy)


def solution(mesh):
    spread = ("groups", "gx")
    return jax.shard_map(
        per_device,
        mesh=mesh,
        in_specs=(
            P(None, spread, "gy", "gz", None),
            P(spread, "gy", "gz", None),
            P(spread, "gy", "gz", None, None),
            P(spread, "gy", "gz", None),
        )
        + (P(),) * 11,
        out_specs=(P(None, spread, "gy", "gz", None), P(spread, "gy", "gz", None)),
        check_vma=False,
    )
```

profile of v0, /device:TPU:0, one launch (start us, length us, event | category | flops | bytes accessed | tf_op | source)
XLA Modules:
  0.0 61.7 jit_solution(2129491460218227407)
XLA Ops:
  0.6 0.0 copy-start
  0.6 1.5 %shard_map.158 = f32[16,8,128]{2,1,0:T(8,128)} custom-call(s32[1,1,1,16]{3,2,1,0:T(1,128)} %send_ref.3, f32[3,1,1,1,128]{4,3,2,1,0:T(1,128)} %pos_ref.1, s32[1,1,1,128]{3,2,1,0:T(1,128)} %species_ref.1, s32[1,1,1,16,128]{4,3,2,1,0:T(8,128)} %neigh_ref.3), custom_call_target="tpu_custom_call" | custom-call | tf_op jit(solution)/shard_map/pallas_call | solution.py:620
  2.2 0.0 copy-start.1
  2.2 7.5 %all-to-all-start = ((f32[16,8,128]{2,1,0:T(8,128)}), f32[16,8,128]{2,1,0:T(8,128)S(1)}, u32[]{:S(2)}, u32[]{:S(2)}) async-start(f32[16,8,128]{2,1,0:T(8,128)} %shard_map.158), calls=%async_computation | async-start | bytes 131072 | tf_op jit(solution)/shard_map/all_to_all | solution.py:628
  9.7 0.0 copy-start.10
  9.7 0.0 copy-start.9
  9.7 0.0 copy-start.7
  9.7 0.0 copy-start.8
  9.7 0.1 pad_add_fusion.base_ref
  9.8 0.0 copy-start.11
  9.8 6.8 %all-to-all-done.table_ref = f32[16,8,128]{2,1,0:T(8,128)S(1)} async-done(((f32[16,8,128]{2,1,0:T(8,128)}), f32[16,8,128]{2,1,0:T(8,128)S(1)}, u32[]{:S(2)}, u32[]{:S(2)}) %all-to-all-start) | async-done | bytes 65568 | tf_op jit(solution)/shard_map/all_to_all | solution.py:628
  16.6 0.0 copy-done
  16.6 0.0 copy-done.1
  16.6 0.0 copy-done.10
  16.6 0.0 copy-done.9
  16.6 0.0 copy-done.7
  16.6 0.0 copy-done.8
  16.6 0.0 copy-done.11
  16.6 0.0 copy-start.2
  16.6 0.8 %copy-done.2 = f32[128,128]{1,0:T(8,128)S(1)} copy-done((f32[128,128]{1,0:T(8,128)S(1)}, f32[128,128]{1,0:T(8,128)}, u32[]{:S(2)}) %copy-start.2) | copy-done | bytes 65560
  17.4 0.0 copy-start.3
  17.4 0.8 %copy-done.3 = f32[128,128]{1,0:T(8,128)S(1)} copy-done((f32[128,128]{1,0:T(8,128)S(1)}, f32[128,128]{1,0:T(8,128)}, u32[]{:S(2)}) %copy-start.3) | copy-done | bytes 65560
  18.3 0.0 copy-start.4
  18.3 0.8 %copy-done.4 = f32[128,128]{1,0:T(8,128)S(1)} copy-done((f32[128,128]{1,0:T(8,128)S(1)}, f32[128,128]{1,0:T(8,128)}, u32[]{:S(2)}) %copy-start.4) | copy-done | bytes 65560
  19.1 0.0 copy-start.5
  19.1 0.8 %copy-done.5 = f32[128,128]{1,0:T(8,128)S(1)} copy-done((f32[128,128]{1,0:T(8,128)S(1)}, f32[128,128]{1,0:T(8,128)}, u32[]{:S(2)}) %copy-start.5) | copy-done | bytes 65560
  20.0 0.0 copy-start.6
  20.0 0.8 %copy-done.6 = f32[128,128]{1,0:T(8,128)S(1)} copy-done((f32[128,128]{1,0:T(8,128)S(1)}, f32[128,128]{1,0:T(8,128)}, u32[]{:S(2)}) %copy-start.6) | copy-done | bytes 65560
  20.8 29.2 %shard_map.159 = (f32[16,8,128]{2,1,0:T(8,128)S(1)}, f32[1,1,1,128]{3,2,1,0:T(1,128)}) custom-call(s32[3]{0:T(128)S(1)} %pad_add_fusion.base_ref, f32[16,8,128]{2,1,0:T(8,128)S(1)} %all-to-all-done.table_ref, s32[1,1,1,16,128]{4,3,2,1,0:T(8,128)S(1)} %copy-done.7, f32[5,128]{1,0:T(8,128)S(1)} %copy-done.8, f32[8,64]{1,0:T(8,128)S(1)} %copy-done.9, ...), custom_call_target="tpu_custom_call" | custom-call | tf_op jit(solution)/shard_map/pallas_call | solution.py:642
  50.0 10.2 %all_to_all.10.parts_ref = f32[16,8,128]{2,1,0:T(8,128)} all-to-all(f32[16,8,128]{2,1,0:T(8,128)S(1)} %get-tuple-element.4), channel_id=1, replica_groups=mesh['groups'=2,'gx'=4,'gy'=2,'gz'=2] {'gx','gy','gz'}, dimensions={0} | all-to-all | bytes 131072 | tf_op jit(solution)/shard_map/all_to_all | solution.py:689
  60.2 1.5 %shard_map.160 = f32[3,1,1,1,128]{4,3,2,1,0:T(1,128)} custom-call(s32[1,1,1,16]{3,2,1,0:T(1,128)} %send_ref.3, f32[16,8,128]{2,1,0:T(8,128)} %all_to_all.10.parts_ref), custom_call_target="tpu_custom_call" | custom-call | tf_op jit(solution)/shard_map/pallas_call | solution.py:701
Async XLA Ops:
  0.6 15.9 %copy-start = (f32[64,512]{1,0:T(8,128)S(1)}, f32[64,512]{1,0:T(8,128)}, u32[]{:S(2)}) copy-start(f32[64,512]{1,0:T(8,128)} %wout_two_ref.1) | copy-start | bytes 393220
  2.2 14.4 %copy-start.1 = (f32[64,256]{1,0:T(8,128)S(1)}, f32[64,256]{1,0:T(8,128)}, u32[]{:S(2)}) copy-start(f32[64,256]{1,0:T(8,128)} %wout_one_ref.1) | copy-start | bytes 196612
  2.2 14.4 %all-to-all-start = ((f32[16,8,128]{2,1,0:T(8,128)}), f32[16,8,128]{2,1,0:T(8,128)S(1)}, u32[]{:S(2)}, u32[]{:S(2)}) async-start(f32[16,8,128]{2,1,0:T(8,128)} %shard_map.158), calls=%async_computation | async-start | bytes 131072 | tf_op jit(solution)/shard_map/all_to_all | solution.py:628
  9.7 6.9 %copy-start.10 = (f32[8,64]{1,0:T(8,128)S(1)}, f32[8,64]{1,0:T(8,128)}, u32[]{:S(2)}) copy-start(f32[8,64]{1,0:T(8,128)} %win_two_ref.1) | copy-start | bytes 6148
  9.7 6.9 %copy-start.9 = (f32[8,64]{1,0:T(8,128)S(1)}, f32[8,64]{1,0:T(8,128)}, u32[]{:S(2)}) copy-start(f32[8,64]{1,0:T(8,128)} %win_one_ref.1) | copy-start | bytes 6148
  9.7 6.9 %copy-start.7 = (s32[1,1,1,16,128]{4,3,2,1,0:T(8,128)S(1)}, s32[1,1,1,16,128]{4,3,2,1,0:T(8,128)}, u32[]{:S(2)}) copy-start(s32[1,1,1,16,128]{4,3,2,1,0:T(8,128)} %neigh_ref.3) | copy-start | bytes 24580
  9.7 6.9 %copy-start.8 = (f32[5,128]{1,0:T(8,128)S(1)}, f32[5,128]{1,0:T(8,128)}, u32[]{:S(2)}) copy-start(f32[5,128]{1,0:T(8,128)} %embedding_ref.1) | copy-start | bytes 7684
  9.8 6.8 %copy-start.11 = (f32[128]{0:T(128)S(1)}, f32[128]{0:T(128)}, u32[]{:S(2)}) copy-start(f32[128]{0:T(128)} %param.29) | copy-start | bytes 1540
  16.6 0.8 %copy-start.2 = (f32[128,128]{1,0:T(8,128)S(1)}, f32[128,128]{1,0:T(8,128)}, u32[]{:S(2)}) copy-start(f32[128,128]{1,0:T(8,128)} %mss_one_ref.1) | copy-start | bytes 196612
  17.4 0.8 %copy-start.3 = (f32[128,128]{1,0:T(8,128)S(1)}, f32[128,128]{1,0:T(8,128)}, u32[]{:S(2)}) copy-start(f32[128,128]{1,0:T(8,128)} %msq_one_ref.1) | copy-start | bytes 196612
  18.3 0.8 %copy-start.4 = (f32[128,128]{1,0:T(8,128)S(1)}, f32[128,128]{1,0:T(8,128)}, u32[]{:S(2)}) copy-start(f32[128,128]{1,0:T(8,128)} %mv_one_ref.1) | copy-start | bytes 196612
  19.1 0.8 %copy-start.5 = (f32[128,128]{1,0:T(8,128)S(1)}, f32[128,128]{1,0:T(8,128)}, u32[]{:S(2)}) copy-start(f32[128,128]{1,0:T(8,128)} %mss_two_ref.1) | copy-start | bytes 196612
  20.0 0.8 %copy-start.6 = (f32[128,128]{1,0:T(8,128)S(1)}, f32[128,128]{1,0:T(8,128)}, u32[]{:S(2)}) copy-start(f32[128,128]{1,0:T(8,128)} %msq_two_ref.1) | copy-start | bytes 196612
where the time goes:
time: 62.2 us; the launch traced here: 61.7 us
  Pallas kernels  32.2 us (52%)
  blocking collectives  10.2 us (16%)
  starting transfers between devices  7.49 us (12%)
  waiting for transfers between devices  6.76 us (11%)
  local copies, waits for them, and re-layouts  4.23 us (7%)
  between operations  0.74 us (1%)
    pallas_call x1, Pallas kernels, per_device(): pl.pallas_call(functools.partial(main_kernel, dims, near), out_shape=(jax...  29.2 us
    all_to_all x1, blocking collectives, per_device(): returned = lax.all_to_all(grads, AXES, 0, 0, tiled=True)  10.2 us
    all_to_all x1, starting transfers between devices, per_device(): table = lax.all_to_all(packed, AXES, 0, 0, tiled=True)  7.49 us
    all_to_all x1, waiting for transfers between devices, per_device(): table = lax.all_to_all(packed, AXES, 0, 0, tiled=True)  6.76 us
    unnamed x24, local copies, waits for them, and re-layouts  4.23 us
    pallas_call x1, Pallas kernels, per_device(): pl.pallas_call(functools.partial(pack_kernel, copies), out_shape=jax.Shap...  1.52 us
    pallas_call x1, Pallas kernels, per_device(): pl.pallas_call(functools.partial(forces_kernel, copies), out_shape=jax.Sh...  1.5 us
  transfers between devices with their start and end apart: 1, of which 1 were waited for; matrix products, arithmetic and copies ran while one was open for 0% of the time, Pallas kernels for 0%

commit v1 on v0

--- a/solution.py
+++ b/solution.py
@@ -14,7 +14,7 @@
 LANES = 128
 GHOSTS = 16
 REACH = 5
-VMEM_BYTES = 52 * 1024 * 1024
+VMEM_BYTES = 60 * 1024 * 1024
 F32 = jnp.float32
 BF16 = jnp.bfloat16
 
@@ -82,7 +82,7 @@
 
 
 def sigmoid(v):
-    return 1.0 / (1.0 + jnp.exp(-v))
+    return 0.5 + 0.5 * jnp.tanh(0.5 * v)
 
 
 def pick_lanes(row, index):
@@ -127,11 +127,34 @@
         out_ref[x, 0, 0] = -(total[x : x + 1] + moved[4 + x : 5 + x])
 
 
-def main_kernel(
+def decay_rates(basis):
+    rates = jnp.zeros((basis, LANES), F32)
+    row = iota((basis, LANES), 0)
+    for m in range(basis):
+        rates = jnp.where(row == m, 0.08 * 2.0 ** (m / 2.0), rates)
+    return rates
+
+
+def ghost_parts(named):
+    ghost = jnp.maximum(named - LANES, 0)
+    block_id, slot = ghost >> 4, ghost & 15
+    first = (block_id * 57) >> 9
+    rest = block_id - first * 9
+    second = (rest * 11) >> 5
+    return [first - 1, second - 1, rest - second * 3 - 1], slot
+
+
+def wide_stack(w):
+    high, low = split(w)
+    return jnp.concatenate([high, low, high], axis=1)
+
+
+def turned_stack(w):
+    return wide_stack(jnp.transpose(w))
+
+
+def prepare_kernel(
     dims,
-    near,
-    base_ref,
-    table_ref,
     neigh_ref,
     embedding_ref,
     win_one_ref,
@@ -144,6 +167,72 @@
     mss_two_ref,
     msq_two_ref,
     readout_ref,
+    pair_ref,
+    basis_ref,
+    slots_ref,
+    pulls_ref,
+    mixes_ref,
+    turns_ref,
+    paths_ref,
+    read_ref,
+):
+    atoms = pair_ref.shape[0]
+    basis, hidden = win_one_ref.shape
+    kinds, channels = embedding_ref.shape
+    near_sizes = [len(near_steps(n)) for n in dims]
+    entries = neigh_ref[0, 0, 0]
+    named = jnp.maximum(entries, 0)
+    shift, slot = ghost_parts(named)
+    steps = [near_place(shift[a], dims[a]) for a in range(3)]
+    order = (steps[0] * near_sizes[1] + steps[1]) * near_sizes[2] + steps[2]
+    row = jnp.where(named < LANES, named, LANES + (order - 1) * GHOSTS + slot)
+    row = jnp.where(entries >= 0, row, -1)
+    position = iota((atoms, LANES), 0)
+    for n in range(16):
+        hot = jnp.where(position == row[n : n + 1], 1.0, 0.0).astype(BF16)
+        pair_ref[:, n * LANES : (n + 1) * LANES] = hot
+
+    rates = decay_rates(basis)
+    for i, win_ref in enumerate((win_one_ref, win_two_ref)):
+        win = win_ref[...]
+        both = jnp.concatenate([win, -rates[:, :hidden] * win], axis=1)
+        high, low = split_wide(both)
+        basis_ref[i] = jnp.concatenate([high, high, low, low], axis=0).astype(BF16)
+    for j in range(2):
+        columns = wout_one_ref[:, j * channels : (j + 1) * channels]
+        rows = [columns * embedding_ref[s : s + 1, :] for s in range(kinds)]
+        combined = jnp.concatenate(rows, axis=0)
+        high, low = split_wide(combined)
+        slots_ref[j] = jnp.transpose(jnp.concatenate([high, low, high], axis=0)).astype(BF16)
+        pulls_ref[j] = wide_stack(combined)
+    pairs = ((mss_one_ref, msq_one_ref), (mss_two_ref, msq_two_ref))
+    for i, (scalar_ref, square_ref) in enumerate(pairs):
+        mixes_ref[i] = jnp.concatenate(
+            [turned_stack(scalar_ref[...]), turned_stack(square_ref[...])], axis=1
+        )
+        turns_ref[2 + 2 * i] = wide_stack(scalar_ref[...])
+        turns_ref[3 + 2 * i] = wide_stack(square_ref[...])
+    turns_ref[0] = turned_stack(mv_one_ref[...])
+    turns_ref[1] = wide_stack(mv_one_ref[...])
+    high, low = split_wide(wout_two_ref[...])
+    paths_ref[...] = jnp.transpose(jnp.concatenate([high, low, high], axis=0)).astype(BF16)
+    read_ref[...] = jnp.transpose(jnp.broadcast_to(readout_ref[...], (LANES, channels)))
+
+
+def main_kernel(
+    dims,
+    near,
+    whole,
+    table_ref,
+    neigh_ref,
+    pair_hbm,
+    basis_hbm,
+    slots_hbm,
+    pulls_hbm,
+    mixes_hbm,
+    turns_hbm,
+    paths_hbm,
+    readout_hbm,
     grad_ref,
     energy_ref,
     r_ref,
@@ -152,36 +241,62 @@
     wh_ref,
     slope_ref,
     wh2_ref,
-    slope2_ref,
     moment_ref,
-    pair_ref,
     target_ref,
     feat_ref,
     source_ref,
     radial_ref,
     node_ref,
     dsource_ref,
-    dradial_ref,
     dr_ref,
     dmoment_ref,
+    pair_ref,
+    basis_ref,
+    slots_ref,
+    pulls_ref,
+    mixes_ref,
+    turns_ref,
+    paths_ref,
+    readout_ref,
+    copy_sem,
 ):
-    nx, ny, nz = dims
+    atoms = pair_hbm.shape[0]
+    moves = {}
+    for i, (name, source, target) in enumerate(
+        (
+            ("basis", basis_hbm, basis_ref),
+            ("slots", slots_hbm, slots_ref),
+            ("mixes", mixes_hbm, mixes_ref),
+            ("turns", turns_hbm, turns_ref),
+            ("high", pair_hbm, pair_ref.at[0:atoms]),
+            ("low", pair_hbm, pair_ref.at[atoms : 2 * atoms]),
+            ("paths", paths_hbm, paths_ref),
+            ("readout", readout_hbm, readout_ref),
+            ("pulls", pulls_hbm, pulls_ref),
+        )
+    ):
+        moves[name] = pltpu.make_async_copy(source, target, copy_sem.at[i])
+        moves[name].start()
+
+    def ready(*names):
+        for name in names:
+            moves.pop(name).wait()
+
     wsize = tuple(window_size(n) for n in dims)
     windows = wsize[0] * wsize[1] * wsize[2]
     halves = -(-windows * GHOSTS // LANES)
     groups = 1 + -(-len(near) // 8)
     channels = LANES
-    kinds = embedding_ref.shape[0]
-    hidden = win_one_ref.shape[1]
-    basis = win_one_ref.shape[0]
+    hidden = paths_ref.shape[1] // 3
+    kinds = pulls_ref.shape[1] // hidden
+    basis = basis_ref.shape[1] // 4
     own_edges = 16 * LANES
-    atoms = groups * LANES
 
     lane16 = iota((16, LANES), 1)
     sub16 = iota((16, LANES), 0)
     lane8 = iota((8, LANES), 1)
     sub8 = iota((8, LANES), 0)
-    bases = [base_ref[a] for a in range(3)]
+    bases = [lax.axis_index(axis) if whole else 0 for axis in AXES]
     near_sizes = [len(near_steps(n)) for n in dims]
 
     def flat(steps):
@@ -226,12 +341,7 @@
         named = jnp.maximum(entries, 0)
         local = named < LANES
         local_index = jnp.where(local, named, 0)
-        ghost = jnp.maximum(named - LANES, 0)
-        block_id, slot = ghost >> 4, ghost & 15
-        first = (block_id * 57) >> 9
-        rest = block_id - first * 9
-        second = (rest * 11) >> 5
-        shift = [first - 1, second - 1, rest - second * 3 - 1]
+        shift, slot = ghost_parts(named)
         sent_index = flat([shift[a] + steps[a] for a in range(3)]) * GHOSTS + slot
         values = []
         for x in range(4):
@@ -261,33 +371,18 @@
                 r_ref[x, g * 16 + n] = jnp.broadcast_to(relative[x][n : n + 1], (8, LANES))
             kind_ref[g * 16 + n] = jnp.broadcast_to(values[3][n : n + 1], (8, LANES))
         if g == 0:
-            steps_near = [near_place(shift[a], dims[a]) for a in range(3)]
-            order = (steps_near[0] * near_sizes[1] + steps_near[1]) * near_sizes[2] + steps_near[2]
-            row = jnp.where(local, local_index, LANES + (order - 1) * GHOSTS + slot)
-            size = atoms
-        else:
-            row = jnp.where(local, local_index, LANES + sent_index)
-            size = LANES + halves * LANES
+            continue
+        row = jnp.where(local, local_index, LANES + sent_index)
+        size = LANES + halves * LANES
         row = jnp.where(valid, row, -1)
         position = iota((size, LANES), 0)
         for n in range(16):
             hot = jnp.where(position == row[n : n + 1], 1.0, 0.0).astype(BF16)
-            if g == 0:
-                pair_ref[0:size, n * LANES : (n + 1) * LANES] = hot
-                pair_ref[size : 2 * size, n * LANES : (n + 1) * LANES] = hot
-            else:
-                target_ref[g - 1, :, n * LANES : (n + 1) * LANES] = hot
-
-    rates = jnp.zeros((basis, LANES), F32)
-    basis_row = iota((basis, LANES), 0)
-    for m in range(basis):
-        rates = jnp.where(basis_row == m, 0.08 * 2.0 ** (m / 2.0), rates)
-
-    def radial_weights(win_ref):
-        win = win_ref[...]
-        both = jnp.concatenate([win, -rates[:, :hidden] * win], axis=1)
-        high, low = split_wide(both)
-        return jnp.concatenate([high, high, low, low], axis=0).astype(BF16)
+            target_ref[g - 1, :, n * LANES : (n + 1) * LANES] = hot
+
+    ready("basis")
+
+    rates = decay_rates(basis)
 
     def radial_rows(weights, octet):
         dist8 = dist_ref[0, pl.ds(octet * 8, 8), :]
@@ -303,16 +398,13 @@
             change = both[hidden:, j * LANES : (j + 1) * LANES]
             gate = sigmoid(before)
             after = before * gate
-            gain = gate * (1.0 + before * (1.0 - gate))
+            gain = gate + after * (1.0 - gate)
             weight = weight8[j : j + 1]
             rows.append((weight * after, slope8[j : j + 1] * after + weight * (gain * change)))
         return rows
 
-    weights_one = radial_weights(win_one_ref)
-    weights_two = radial_weights(win_two_ref)
-
     def radial_one_step(octet, carry):
-        for j, (value, slope) in enumerate(radial_rows(weights_one, octet)):
+        for j, (value, slope) in enumerate(radial_rows(basis_ref[0], octet)):
             wh_ref[octet * 8 + j] = value
             slope_ref[octet * 8 + j] = slope
         return carry
@@ -320,56 +412,47 @@
     lax.fori_loop(0, groups * 2, radial_one_step, 0)
 
     def radial_two_step(octet, carry):
-        rows = radial_rows(weights_two, octet)
+        rows = radial_rows(basis_ref[1], octet)
         lanes = pl.ds(pl.multiple_of(octet * 8 * LANES, 8 * LANES), 8 * LANES)
-        stack = data_stack(jnp.concatenate([value for value, _ in rows], axis=1))
-        wh2_ref[:, lanes] = stack
-        for j, (_, slope) in enumerate(rows):
-            slope2_ref[octet * 8 + j] = slope
+        for i in range(2):
+            wh2_ref[i, :, lanes] = data_stack(jnp.concatenate([row[i] for row in rows], axis=1))
         return carry
 
     lax.fori_loop(0, 2, radial_two_step, 0)
 
     def moment_step(step, carry):
-        g, part = step // (hidden // 8), step % (hidden // 8)
-        rows = pl.ds(pl.multiple_of(part * 8, 8), 8)
+        g, part = step // (hidden // 16), step % (hidden // 16)
         lanes = pl.ds(pl.multiple_of(g * LANES, LANES), LANES)
-        sums = [[jnp.zeros((8, LANES), F32) for _ in range(4)] for _ in range(kinds)]
+        sums = [[[jnp.zeros((8, LANES), F32) for _ in range(4)] for _ in range(kinds)] for _ in range(2)]
         for n in range(16):
             e = g * 16 + n
-            value = wh_ref[e, rows, :]
-            parts = [value] + [value * r_ref[x, e] for x in range(3)]
             kind = kind_ref[e]
+            masks = [kind == float(s) for s in range(kinds)]
+            for i in range(2):
+                value = wh_ref[e, pl.ds(pl.multiple_of(part * 16 + i * 8, 8), 8), :]
+                parts = [value] + [value * r_ref[x, e] for x in range(3)]
+                for s in range(kinds):
+                    for j in range(4):
+                        sums[i][s][j] = sums[i][s][j] + jnp.where(masks[s], parts[j], 0.0)
+        for i in range(2):
             for s in range(kinds):
-                mask = kind == float(s)
+                place = pl.ds(pl.multiple_of(s * hidden + part * 16 + i * 8, 8), 8)
                 for j in range(4):
-                    sums[s][j] = sums[s][j] + jnp.where(mask, parts[j], 0.0)
-        for s in range(kinds):
-            for j in range(4):
-                place = pl.ds(pl.multiple_of(s * hidden + part * 8, 8), 8)
-                moment_ref[j, place, lanes] = sums[s][j]
+                    moment_ref[j, place, lanes] = sums[i][s][j]
         return carry
 
-    lax.fori_loop(0, groups * (hidden // 8), moment_step, 0)
-
-    wout_one = wout_one_ref[...]
-    combined = []
-    for j in range(2):
-        columns = wout_one[:, j * channels : (j + 1) * channels]
-        rows = [columns * embedding_ref[s : s + 1, :] for s in range(kinds)]
-        combined.append(jnp.concatenate(rows, axis=0))
-    stacked_weights = [weight_stack(w) for w in combined]
-    scalar_one = dot_tn(stacked_weights[0], data_stack(moment_ref[0]))
-    vector_one = [dot_tn(stacked_weights[1], data_stack(moment_ref[1 + x])) for x in range(3)]
+    lax.fori_loop(0, groups * (hidden // 16), moment_step, 0)
+
+    ready("slots", "mixes", "turns")
+
+    scalar_one = dot_nn(slots_ref[0], data_stack(moment_ref[0]))
+    vector_one = [dot_nn(slots_ref[1], data_stack(moment_ref[1 + x])) for x in range(3)]
     squares_one = sum(v * v for v in vector_one)
-    mss_one, msq_one, mv_one = mss_one_ref[...], msq_one_ref[...], mv_one_ref[...]
-    mix_one = jnp.concatenate([weight_stack(mss_one), weight_stack(msq_one)], axis=0)
-    before_one = dot_tn(
-        mix_one, jnp.concatenate([data_stack(scalar_one), data_stack(squares_one)], axis=0)
+    before_one = dot_nn(
+        mixes_ref[0], jnp.concatenate([data_stack(scalar_one), data_stack(squares_one)], axis=0)
     )
     gate_one = sigmoid(before_one)
-    mv_stack = weight_stack(mv_one)
-    features = [before_one * gate_one] + [dot_tn(mv_stack, data_stack(v)) for v in vector_one]
+    features = [before_one * gate_one] + [dot_nn(turns_ref[0], data_stack(v)) for v in vector_one]
     gain_one = gate_one * (1.0 + before_one * (1.0 - gate_one))
     for j in range(4):
         rows = slice(j * channels, (j + 1) * channels)
@@ -378,14 +461,13 @@
     for x in range(3):
         node_ref[5 + x, :, 0:atoms] = vector_one[x]
 
-    wout_two = wout_two_ref[...]
-    wout_two_high, wout_two_low = split(wout_two)
-    radial_stack = jnp.concatenate([wout_two_high, wout_two_low, wout_two_high], axis=0)
+    ready("high", "low", "paths")
 
     def edge_step(step, carry):
         lanes = pl.ds(pl.multiple_of(step * 256, 256), 256)
         source_ref[:, lanes] = dot_nn(feat_ref[...], pair_ref[:, lanes])
-        radial_ref[:, lanes] = dot_tn(radial_stack, wh2_ref[:, lanes])
+        for i in range(2):
+            radial_ref[i, :, lanes] = dot_nn(paths_ref[...], wh2_ref[i, :, lanes])
         return carry
 
     lax.fori_loop(0, own_edges // 256, edge_step, 0)
@@ -399,7 +481,7 @@
             lanes = slice(n * LANES, (n + 1) * LANES)
             t = source_ref[rows(0), lanes]
             u = [source_ref[rows(1 + x), lanes] for x in range(3)]
-            paths = [radial_ref[rows(j), lanes] for j in range(4)]
+            paths = [radial_ref[0, rows(j), lanes] for j in range(4)]
             r = [r_ref[x, n] for x in range(3)]
             along = r[0] * u[0] + r[1] * u[1] + r[2] * u[2]
             sums[0] = sums[0] + (paths[0] * t + paths[1] * along)
@@ -412,20 +494,21 @@
 
     lax.fori_loop(0, channels // 8, sum_step, 0)
 
+    ready("readout", "pulls")
+
     scalar_two = node_ref[0, :, 0:LANES]
     vector_two = [node_ref[1 + x, :, 0:LANES] for x in range(3)]
     squares_two = sum(v * v for v in vector_two)
-    mss_two, msq_two = mss_two_ref[...], msq_two_ref[...]
-    mix_two = jnp.concatenate([weight_stack(mss_two), weight_stack(msq_two)], axis=0)
-    before_two = dot_tn(
-        mix_two, jnp.concatenate([data_stack(scalar_two), data_stack(squares_two)], axis=0)
+    before_two = dot_nn(
+        mixes_ref[1], jnp.concatenate([data_stack(scalar_two), data_stack(squares_two)], axis=0)
     )
     gate_two = sigmoid(before_two)
-    readout = jnp.transpose(jnp.broadcast_to(readout_ref[...], (LANES, channels)))
+    readout = readout_ref[...]
     energy_ref[0, 0] = jnp.sum(readout * (before_two * gate_two), axis=0, keepdims=True)
     dbefore_two = readout * (gate_two * (1.0 + before_two * (1.0 - gate_two)))
-    dscalar_two = product_nn(*split(mss_two), dbefore_two)
-    dsquares_two = product_nn(*split(msq_two), dbefore_two)
+    dbefore_two = data_stack(dbefore_two)
+    dscalar_two = dot_nn(turns_ref[4], dbefore_two)
+    dsquares_two = dot_nn(turns_ref[5], dbefore_two)
     node_ref[0, :, 0:LANES] = dscalar_two
     for x in range(3):
         node_ref[1 + x, :, 0:LANES] = 2.0 * vector_two[x] * dsquares_two
@@ -433,7 +516,7 @@
     def back_step(n, carry):
         lanes = pl.ds(pl.multiple_of(n * LANES, LANES), LANES)
         r = [jnp.concatenate([r_ref[x, n]] * 2, axis=0) for x in range(3)]
-        totals = [jnp.zeros((16, LANES), F32) for _ in range(3)]
+        totals = [jnp.zeros((16, LANES), F32) for _ in range(4)]
         for part in range(channels // 16):
 
             def rows(j):
@@ -441,7 +524,7 @@
 
             t = source_ref[rows(0), lanes]
             u = [source_ref[rows(1 + x), lanes] for x in range(3)]
-            paths = [radial_ref[rows(j), lanes] for j in range(4)]
+            paths = [radial_ref[0, rows(j), lanes] for j in range(4)]
             ds = node_ref[0, rows(0), 0:LANES]
             dv = [node_ref[1 + x, rows(0), 0:LANES] for x in range(3)]
             push = paths[1] * ds
@@ -454,48 +537,33 @@
                 dsource.append(push * r[x] + paths[3] * dv[x])
                 totals[x] = totals[x] + (push * u[x] + turned * dv[x])
             dradial = [ds * t, ds * along, t * facing, meeting]
+            slopes = [radial_ref[1, rows(j), lanes] for j in range(4)]
+            products = [dradial[j] * slopes[j] for j in range(4)]
+            totals[3] = totals[3] + ((products[0] + products[1]) + (products[2] + products[3]))
             for j in range(4):
                 dsource_ref[0, rows(j), lanes], dsource_ref[1, rows(j), lanes] = split(dsource[j])
-                dradial_ref[0, rows(j), lanes], dradial_ref[1, rows(j), lanes] = split(dradial[j])
+        dd = 2.0 * jnp.sum(totals[3], axis=0, keepdims=True)
         for x in range(3):
             total = jnp.sum(totals[x], axis=0, keepdims=True)
-            dr_ref[x : x + 1, lanes] = total
+            dr_ref[x : x + 1, lanes] = total + dd * r_ref[x, n, 0:1, :]
         return carry
 
     lax.fori_loop(0, 16, back_step, 0)
 
-    dfeat = dot_nt(dsource_ref[0], pair_ref[0:atoms, :]) + dot_nt(
+    source_ref[:, 0:atoms] = dot_nt(dsource_ref[0], pair_ref[0:atoms, :]) + dot_nt(
         dsource_ref[1], pair_ref[0:atoms, :]
     )
-
-    def radial_back_step(step, carry):
-        lanes = pl.ds(pl.multiple_of(step * 512, 512), 512)
-        dhigh, dlow = dradial_ref[0, :, lanes], dradial_ref[1, :, lanes]
-        dwh = dot_nn(wout_two_high, dhigh) + dot_nn(wout_two_low, dhigh) + dot_nn(wout_two_high, dlow)
-        for j in range(4):
-            n = step * 4 + j
-            dd = jnp.sum(
-                dwh[:, j * LANES : (j + 1) * LANES] * slope2_ref[n], axis=0, keepdims=True
-            )
-            at = pl.ds(pl.multiple_of(n * LANES, LANES), LANES)
-            for x in range(3):
-                dr_ref[x : x + 1, at] = dr_ref[x : x + 1, at] + 2.0 * dd * r_ref[x, n, 0:1, :]
-        return carry
-
-    lax.fori_loop(0, 4, radial_back_step, 0)
-
+    dfeat = source_ref[:, 0:atoms]
     gain_one = node_ref[4, :, 0:atoms]
     vector_one = [node_ref[5 + x, :, 0:atoms] for x in range(3)]
-    dbefore_one = dfeat[0:channels] * gain_one
-    dscalar_one = product_nn(*split(mss_one), dbefore_one)
-    dsquares_one = product_nn(*split(msq_one), dbefore_one)
-    mv_parts = split(mv_one)
-    dmoment_ref[0] = product_nn(*split(combined[0]), dscalar_one)
-    combined_parts = split(combined[1])
+    dbefore_one = data_stack(dfeat[0:channels] * gain_one)
+    dscalar_one = dot_nn(turns_ref[2], dbefore_one)
+    dsquares_one = dot_nn(turns_ref[3], dbefore_one)
+    dmoment_ref[0] = dot_nn(pulls_ref[0], data_stack(dscalar_one))
     for x in range(3):
-        du = dfeat[(1 + x) * channels : (2 + x) * channels]
-        dvector = 2.0 * vector_one[x] * dsquares_one + product_nn(*mv_parts, du)
-        dmoment_ref[1 + x] = product_nn(*combined_parts, dvector)
+        du = data_stack(dfeat[(1 + x) * channels : (2 + x) * channels])
+        dvector = 2.0 * vector_one[x] * dsquares_one + dot_nn(turns_ref[1], du)
+        dmoment_ref[1 + x] = dot_nn(pulls_ref[1], data_stack(dvector))
 
     def one_back_step(step, carry):
         g = step // 4
@@ -626,7 +694,6 @@
 
     if whole:
         table = lax.all_to_all(packed, AXES, 0, 0, tiled=True)
-        base = jnp.stack([lax.axis_index(axis) for axis in AXES]).astype(jnp.int32)
     else:
         table = packed.reshape(1, 1, 1, 8, LANES)
         for dim, axis in reversed(list(enumerate(AXES))):
@@ -635,43 +702,8 @@
             ]
             table = jnp.concatenate(parts, axis=dim)
         table = table.reshape(windows, 8, LANES)
-        base = jnp.zeros((3,), jnp.int32)
-
-    rows = groups * 16
-    edges = 16 * LANES
-    grads, energy = pl.pallas_call(
-        functools.partial(main_kernel, dims, near),
-        out_shape=(
-            jax.ShapeDtypeStruct((windows, 8, LANES), F32),
-            jax.ShapeDtypeStruct((1, 1, 1, LANES), F32),
-        ),
-        in_specs=[smem] + [vmem] * 13,
-        out_specs=(vmem, vmem),
-        scratch_shapes=[
-            pltpu.VMEM((3, rows, 8, LANES), F32),
-            pltpu.VMEM((rows, 8, LANES), F32),
-            pltpu.VMEM((3, rows, LANES), F32),
-            pltpu.VMEM((rows, hidden, LANES), F32),
-            pltpu.VMEM((rows, hidden, LANES), F32),
-            pltpu.VMEM((3 * hidden, edges), BF16),
-            pltpu.VMEM((16, hidden, LANES), F32),
-            pltpu.VMEM((4, kinds * hidden, atoms), F32),
-            pltpu.VMEM((2 * atoms, edges), BF16),
-            pltpu.VMEM((groups - 1, LANES + halves * LANES, edges), BF16),
-            pltpu.VMEM((4 * channels, 2 * atoms), BF16),
-            pltpu.VMEM((4 * channels, edges), F32),
-            pltpu.VMEM((4 * channels, edges), F32),
-            pltpu.VMEM((8, channels, atoms), F32),
-            pltpu.VMEM((2, 4 * channels, edges), BF16),
-            pltpu.VMEM((2, 4 * channels, edges), BF16),
-            pltpu.VMEM((8, rows * LANES), F32),
-            pltpu.VMEM((4, kinds * hidden, atoms), F32),
-        ],
-        compiler_params=pltpu.CompilerParams(vmem_limit_bytes=VMEM_BYTES),
-    )(
-        base,
-        table,
-        neighbours,
+
+    weights = (
         embedding,
         radial_in,
         radial_out_one,
@@ -684,6 +716,55 @@
         mix_square_two,
         readout.reshape(1, channels),
     )
+    rows = groups * 16
+    edges = 16 * LANES
+    prepared = pl.pallas_call(
+        functools.partial(prepare_kernel, dims),
+        out_shape=(
+            jax.ShapeDtypeStruct((atoms, edges), BF16),
+            jax.ShapeDtypeStruct((2, 4 * radial_in.shape[0], 2 * hidden), BF16),
+            jax.ShapeDtypeStruct((2, channels, 3 * kinds * hidden), BF16),
+            jax.ShapeDtypeStruct((2, kinds * hidden, 3 * channels), BF16),
+            jax.ShapeDtypeStruct((2, channels, 6 * channels), BF16),
+            jax.ShapeDtypeStruct((6, channels, 3 * channels), BF16),
+            jax.ShapeDtypeStruct((4 * channels, 3 * hidden), BF16),
+            jax.ShapeDtypeStruct((channels, LANES), F32),
+        ),
+        in_specs=[vmem] * 12,
+        out_specs=(vmem,) * 8,
+        compiler_params=pltpu.CompilerParams(vmem_limit_bytes=VMEM_BYTES),
+        cost_estimate=pl.CostEstimate(flops=0, bytes_accessed=8 * 1024 * 1024, transcendentals=0),
+    )(neighbours, *weights)
+    grads, energy = pl.pallas_call(
+        functools.partial(main_kernel, dims, near, whole),
+        out_shape=(
+            jax.ShapeDtypeStruct((windows, 8, LANES), F32),
+            jax.ShapeDtypeStruct((1, 1, 1, LANES), F32),
+        ),
+        in_specs=[vmem] * 2 + [pl.BlockSpec(memory_space=pltpu.HBM)] * len(prepared),
+        out_specs=(vmem, vmem),
+        scratch_shapes=[
+            pltpu.VMEM((3, rows, 8, LANES), F32),
+            pltpu.VMEM((rows, 8, LANES), F32),
+            pltpu.VMEM((3, rows, LANES), F32),
+            pltpu.VMEM((rows, hidden, LANES), F32),
+            pltpu.VMEM((rows, hidden, LANES), F32),
+            pltpu.VMEM((2, 3 * hidden, edges), BF16),
+            pltpu.VMEM((4, kinds * hidden, atoms), F32),
+            pltpu.VMEM((groups - 1, LANES + halves * LANES, edges), BF16),
+            pltpu.VMEM((4 * channels, 2 * atoms), BF16),
+            pltpu.VMEM((4 * channels, edges), F32),
+            pltpu.VMEM((2, 4 * channels, edges), F32),
+            pltpu.VMEM((8, channels, atoms), F32),
+            pltpu.VMEM((2, 4 * channels, edges), BF16),
+            pltpu.VMEM((8, rows * LANES), F32),
+            pltpu.VMEM((4, kinds * hidden, atoms), F32),
+            pltpu.VMEM((2 * atoms, edges), BF16),
+        ]
+        + [pltpu.VMEM(p.shape, p.dtype) for p in prepared[1:]]
+        + [pltpu.SemaphoreType.DMA((len(prepared) + 1,))],
+        compiler_params=pltpu.CompilerParams(vmem_limit_bytes=VMEM_BYTES),
+    )(table, neighbours, *prepared)
 
     if whole:
         returned = lax.all_to_all(grads, AXES, 0, 0, tiled=True)

time: 62.2 us -> 56.8 us (0.913)
  local copies, waits for them, and re-layouts: 4.23 us -> 0.63 us
  waiting for transfers between devices: 6.76 us -> 3.39 us
  Pallas kernels: 32.2 us -> 33.3 us
  blocking collectives: 10.2 us -> 11 us
    unnamed x24 -> x2, local copies, waits for them, and re-layouts: 4.23 us -> 0.63 us
    all_to_all x1, waiting for transfers between devices: 6.76 us -> 3.39 us  [per_device(): table = lax.all_to_all(packed, AXES, 0, 0, tiled=True)]
    pallas_call x1 -> x2, Pallas kernels: 29.2 us -> 30.3 us  [the longest x1 26.8 us: per_device(): pl.pallas_call(functools.partial(main_kernel, dims, near, whole), out_sha...]
    all_to_all x1, blocking collectives: 10.2 us -> 11 us  [per_device(): returned = lax.all_to_all(grads, AXES, 0, 0, tiled=True)]
  transfers between devices with their start and end apart: 1 -> 1, of which waited for: 1 -> 1; matrix products, arithmetic and copies ran while one was open for 0% -> 0% of each run, Pallas kernels for 0% -> 6%
where the time goes in v1:
time: 56.8 us; the launch traced here: 56.4 us
  Pallas kernels  33.3 us (59%)
  blocking collectives  11 us (19%)
  starting transfers between devices  7.36 us (13%)
  waiting for transfers between devices  3.39 us (6%)
  between operations  0.65 us (1%)
  local copies, waits for them, and re-layouts  0.63 us (1%)
    pallas_call x1, Pallas kernels, per_device(): pl.pallas_call(functools.partial(main_kernel, dims, near, whole), out_sha...  26.8 us
    all_to_all x1, blocking collectives, per_device(): returned = lax.all_to_all(grads, AXES, 0, 0, tiled=True)  11 us
    all_to_all x1, starting transfers between devices, per_device(): table = lax.all_to_all(packed, AXES, 0, 0, tiled=True)  7.36 us
    pallas_call x1, Pallas kernels, per_device(): pl.pallas_call(functools.partial(prepare_kernel, dims), out_shape=(jax.Sh...  3.5 us
    all_to_all x1, waiting for transfers between devices, per_device(): table = lax.all_to_all(packed, AXES, 0, 0, tiled=True)  3.39 us
    pallas_call x1, Pallas kernels, per_device(): pl.pallas_call(functools.partial(pack_kernel, copies), out_shape=jax.Shap...  1.52 us
    pallas_call x1, Pallas kernels, per_device(): pl.pallas_call(functools.partial(forces_kernel, copies), out_shape=jax.Sh...  1.5 us
  transfers between devices with their start and end apart: 1, of which 1 were waited for; matrix products, arithmetic and copies ran while one was open for 0% of the time, Pallas kernels for 6%

profile of v1, /device:TPU:0, one launch (start us, length us, event | category | flops | bytes accessed | tf_op | source)
XLA Modules:
  0.0 56.4 jit_solution(5052137565785702833)
XLA Ops:
  0.6 1.5 %shard_map.158 = f32[16,8,128]{2,1,0:T(8,128)} custom-call(s32[1,1,1,16]{3,2,1,0:T(1,128)} %send_ref.3, f32[3,1,1,1,128]{4,3,2,1,0:T(1,128)} %pos_ref.1, s32[1,1,1,128]{3,2,1,0:T(1,128)} %species_ref.1, s32[1,1,1,16,128]{4,3,2,1,0:T(8,128)} %neigh_ref.5), custom_call_target="tpu_custom_call" | custom-call | tf_op jit(solution)/shard_map/pallas_call | solution.py:688
  2.1 7.4 %all-to-all-start = ((f32[16,8,128]{2,1,0:T(8,128)}), f32[16,8,128]{2,1,0:T(8,128)S(1)}, u32[]{:S(2)}, u32[]{:S(2)}) async-start(f32[16,8,128]{2,1,0:T(8,128)} %shard_map.158), calls=%async_computation | async-start | bytes 131072 | tf_op jit(solution)/shard_map/all_to_all | solution.py:696
  9.5 3.5 %shard_map.159 = (bf16[384,2048]{1,0:T(8,128)(2,1)}, bf16[2,32,128]{2,1,0:T(8,128)(2,1)}, bf16[2,128,960]{2,1,0:T(8,128)(2,1)}, bf16[2,320,384]{2,1,0:T(8,128)(2...) custom-call(s32[1,1,1,16,128]{4,3,2,1,0:T(8,128)} %neigh_ref.5, ...), custom_call_target="tpu_custom_call" | custom-call | bytes 8388608 | tf_op jit(solution)/shard_map/pallas_call | solution.py:721
  13.0 3.4 %all-to-all-done.table_ref = f32[16,8,128]{2,1,0:T(8,128)S(1)} async-done(((f32[16,8,128]{2,1,0:T(8,128)}), f32[16,8,128]{2,1,0:T(8,128)S(1)}, u32[]{:S(2)}, u32[]{:S(2)}) %all-to-all-start) | async-done | bytes 65568 | tf_op jit(solution)/shard_map/all_to_all | solution.py:696
  16.4 0.0 copy-start
  16.4 0.6 %copy-done = f32[16,8,128]{2,1,0:T(8,128)} copy-done((f32[16,8,128]{2,1,0:T(8,128)}, f32[16,8,128]{2,1,0:T(8,128)S(1)}, u32[]{:S(2)}) %copy-start) | copy-done | bytes 65560
  17.0 26.8 %shard_map.160 = (f32[16,8,128]{2,1,0:T(8,128)}, f32[1,1,1,128]{3,2,1,0:T(1,128)}) custom-call(f32[16,8,128]{2,1,0:T(8,128)} %copy-done, s32[1,1,1,16,128]{4,3,2,1,0:T(8,128)} %neigh_ref.5, bf16[384,2048]{1,0:T(8,128)(2,1)} %get-tuple-element.12.pair_hbm, bf16[2,32,128]{2,1,0:T(8,128)(2,1)} %get-tuple-element.13.basis_hbm, ...), custom_call_target="tpu_custom_call" | custom-call | tf_op jit(solution)/shard_map/pallas_call | solution.py:738
  43.8 11.0 %all_to_all.10.parts_ref = f32[16,8,128]{2,1,0:T(8,128)} all-to-all(f32[16,8,128]{2,1,0:T(8,128)} %get-tuple-element.20), channel_id=1, replica_groups=mesh['groups'=2,'gx'=4,'gy'=2,'gz'=2] {'gx','gy','gz'}, dimensions={0} | all-to-all | bytes 131072 | tf_op jit(solution)/shard_map/all_to_all | solution.py:770
  54.9 1.5 %shard_map.161 = f32[3,1,1,1,128]{4,3,2,1,0:T(1,128)} custom-call(s32[1,1,1,16]{3,2,1,0:T(1,128)} %send_ref.3, f32[16,8,128]{2,1,0:T(8,128)} %all_to_all.10.parts_ref), custom_call_target="tpu_custom_call" | custom-call | tf_op jit(solution)/shard_map/pallas_call | solution.py:782
Async XLA Ops:
  2.1 14.3 %all-to-all-start = ((f32[16,8,128]{2,1,0:T(8,128)}), f32[16,8,128]{2,1,0:T(8,128)S(1)}, u32[]{:S(2)}, u32[]{:S(2)}) async-start(f32[16,8,128]{2,1,0:T(8,128)} %shard_map.158), calls=%async_computation | async-start | bytes 131072 | tf_op jit(solution)/shard_map/all_to_all | solution.py:696
  16.4 0.6 %copy-start = (f32[16,8,128]{2,1,0:T(8,128)}, f32[16,8,128]{2,1,0:T(8,128)S(1)}, u32[]{:S(2)}) copy-start(f32[16,8,128]{2,1,0:T(8,128)S(1)} %all-to-all-done.table_ref) | copy-start | bytes 196612

commit v2 on v1

--- a/solution.py
+++ b/solution.py
@@ -15,6 +15,7 @@
 GHOSTS = 16
 REACH = 5
 VMEM_BYTES = 60 * 1024 * 1024
+MAIN_BYTES = 55040 * 1024
 F32 = jnp.float32
 BF16 = jnp.bfloat16
 
@@ -168,13 +169,11 @@
     msq_two_ref,
     readout_ref,
     pair_ref,
-    basis_ref,
     slots_ref,
     pulls_ref,
     mixes_ref,
     turns_ref,
     paths_ref,
-    read_ref,
 ):
     atoms = pair_ref.shape[0]
     basis, hidden = win_one_ref.shape
@@ -197,7 +196,8 @@
         win = win_ref[...]
         both = jnp.concatenate([win, -rates[:, :hidden] * win], axis=1)
         high, low = split_wide(both)
-        basis_ref[i] = jnp.concatenate([high, high, low, low], axis=0).astype(BF16)
+        stack = jnp.concatenate([high, high, low, low], axis=0).astype(BF16)
+        turns_ref[6, i * 4 * basis : (i + 1) * 4 * basis, 0 : 2 * hidden] = stack
     for j in range(2):
         columns = wout_one_ref[:, j * channels : (j + 1) * channels]
         rows = [columns * embedding_ref[s : s + 1, :] for s in range(kinds)]
@@ -216,23 +216,24 @@
     turns_ref[1] = wide_stack(mv_one_ref[...])
     high, low = split_wide(wout_two_ref[...])
     paths_ref[...] = jnp.transpose(jnp.concatenate([high, low, high], axis=0)).astype(BF16)
-    read_ref[...] = jnp.transpose(jnp.broadcast_to(readout_ref[...], (LANES, channels)))
+    read = jnp.transpose(jnp.broadcast_to(readout_ref[...], (LANES, channels)))
+    turns_ref[6, :, LANES : 2 * LANES], turns_ref[6, :, 2 * LANES : 3 * LANES] = split(read)
+    turns_ref[6, 8 * basis : channels, 0:LANES] = jnp.zeros((channels - 8 * basis, LANES), BF16)
 
 
 def main_kernel(
     dims,
     near,
     whole,
+    rank,
     table_ref,
     neigh_ref,
     pair_hbm,
-    basis_hbm,
     slots_hbm,
     pulls_hbm,
     mixes_hbm,
     turns_hbm,
     paths_hbm,
-    readout_hbm,
     grad_ref,
     energy_ref,
     r_ref,
@@ -251,27 +252,25 @@
     dr_ref,
     dmoment_ref,
     pair_ref,
-    basis_ref,
     slots_ref,
     pulls_ref,
     mixes_ref,
     turns_ref,
     paths_ref,
-    readout_ref,
     copy_sem,
+    place_ref,
+    dfeat_ref,
 ):
     atoms = pair_hbm.shape[0]
     moves = {}
     for i, (name, source, target) in enumerate(
         (
-            ("basis", basis_hbm, basis_ref),
+            ("turns", turns_hbm, turns_ref),
             ("slots", slots_hbm, slots_ref),
             ("mixes", mixes_hbm, mixes_ref),
-            ("turns", turns_hbm, turns_ref),
             ("high", pair_hbm, pair_ref.at[0:atoms]),
             ("low", pair_hbm, pair_ref.at[atoms : 2 * atoms]),
             ("paths", paths_hbm, paths_ref),
-            ("readout", readout_hbm, readout_ref),
             ("pulls", pulls_hbm, pulls_ref),
         )
     ):
@@ -289,7 +288,7 @@
     channels = LANES
     hidden = paths_ref.shape[1] // 3
     kinds = pulls_ref.shape[1] // hidden
-    basis = basis_ref.shape[1] // 4
+    basis = rank
     own_edges = 16 * LANES
 
     lane16 = iota((16, LANES), 1)
@@ -373,21 +372,16 @@
         if g == 0:
             continue
         row = jnp.where(local, local_index, LANES + sent_index)
-        size = LANES + halves * LANES
-        row = jnp.where(valid, row, -1)
-        position = iota((size, LANES), 0)
-        for n in range(16):
-            hot = jnp.where(position == row[n : n + 1], 1.0, 0.0).astype(BF16)
-            target_ref[g - 1, :, n * LANES : (n + 1) * LANES] = hot
-
-    ready("basis")
+        place_ref[g - 1] = jnp.where(valid, row, -1)
+
+    ready("turns")
 
     rates = decay_rates(basis)
 
     def radial_rows(weights, octet):
-        dist8 = dist_ref[0, pl.ds(octet * 8, 8), :]
-        weight8 = dist_ref[1, pl.ds(octet * 8, 8), :]
-        slope8 = dist_ref[2, pl.ds(octet * 8, 8), :]
+        dist8 = dist_ref[0, octet * 8 : octet * 8 + 8, :]
+        weight8 = dist_ref[1, octet * 8 : octet * 8 + 8, :]
+        slope8 = dist_ref[2, octet * 8 : octet * 8 + 8, :]
         values = jnp.concatenate([jnp.exp(-rates * dist8[j : j + 1]) for j in range(8)], axis=1)
         high, low = split_wide(values)
         stacked = jnp.concatenate([high, low, high, low], axis=0).astype(BF16)
@@ -404,21 +398,23 @@
         return rows
 
     def radial_one_step(octet, carry):
-        for j, (value, slope) in enumerate(radial_rows(basis_ref[0], octet)):
+        for j, (value, slope) in enumerate(radial_rows(turns_ref[6, 0 : 4 * basis, 0 : 2 * hidden], octet)):
             wh_ref[octet * 8 + j] = value
             slope_ref[octet * 8 + j] = slope
         return carry
 
-    lax.fori_loop(0, groups * 2, radial_one_step, 0)
+    for octet in range(groups * 2):
+        radial_one_step(octet, 0)
 
     def radial_two_step(octet, carry):
-        rows = radial_rows(basis_ref[1], octet)
-        lanes = pl.ds(pl.multiple_of(octet * 8 * LANES, 8 * LANES), 8 * LANES)
+        rows = radial_rows(turns_ref[6, 4 * basis : 8 * basis, 0 : 2 * hidden], octet)
+        lanes = slice(octet * 8 * LANES, (octet + 1) * 8 * LANES)
         for i in range(2):
             wh2_ref[i, :, lanes] = data_stack(jnp.concatenate([row[i] for row in rows], axis=1))
         return carry
 
-    lax.fori_loop(0, 2, radial_two_step, 0)
+    for octet in range(2):
+        radial_two_step(octet, 0)
 
     def moment_step(step, carry):
         g, part = step // (hidden // 16), step % (hidden // 16)
@@ -443,7 +439,7 @@
 
     lax.fori_loop(0, groups * (hidden // 16), moment_step, 0)
 
-    ready("slots", "mixes", "turns")
+    ready("slots", "mixes")
 
     scalar_one = dot_nn(slots_ref[0], data_stack(moment_ref[0]))
     vector_one = [dot_nn(slots_ref[1], data_stack(moment_ref[1 + x])) for x in range(3)]
@@ -464,37 +460,48 @@
     ready("high", "low", "paths")
 
     def edge_step(step, carry):
-        lanes = pl.ds(pl.multiple_of(step * 256, 256), 256)
+        lanes = slice(step * 256, step * 256 + 256)
         source_ref[:, lanes] = dot_nn(feat_ref[...], pair_ref[:, lanes])
         for i in range(2):
             radial_ref[i, :, lanes] = dot_nn(paths_ref[...], wh2_ref[i, :, lanes])
+        position = iota((LANES + halves * LANES, LANES), 0)
+        for i in range(2):
+            n = step * 2 + i
+            at = slice(n * LANES, n * LANES + LANES)
+            for g in range(groups - 1):
+                hot = position == place_ref[g, n : n + 1, :]
+                target_ref[g, :, at] = jnp.where(hot, 1.0, 0.0).astype(BF16)
         return carry
 
-    lax.fori_loop(0, own_edges // 256, edge_step, 0)
-
-    def sum_step(part, carry):
-        def rows(j):
-            return pl.ds(pl.multiple_of(j * channels + part * 8, 8), 8)
-
-        sums = [jnp.zeros((8, LANES), F32) for _ in range(4)]
-        for n in range(16):
-            lanes = slice(n * LANES, (n + 1) * LANES)
-            t = source_ref[rows(0), lanes]
-            u = [source_ref[rows(1 + x), lanes] for x in range(3)]
-            paths = [radial_ref[0, rows(j), lanes] for j in range(4)]
-            r = [r_ref[x, n] for x in range(3)]
-            along = r[0] * u[0] + r[1] * u[1] + r[2] * u[2]
-            sums[0] = sums[0] + (paths[0] * t + paths[1] * along)
-            turned = paths[2] * t
-            for x in range(3):
-                sums[1 + x] = sums[1 + x] + (turned * r[x] + paths[3] * u[x])
-        for j in range(4):
-            node_ref[j, pl.ds(pl.multiple_of(part * 8, 8), 8), 0:LANES] = sums[j]
-        return carry
-
-    lax.fori_loop(0, channels // 8, sum_step, 0)
-
-    ready("readout", "pulls")
+    def sum_slots(step):
+        for part in range(channels // 8):
+
+            def rows(j):
+                return slice(j * channels + part * 8, j * channels + part * 8 + 8)
+
+            sums = [node_ref[j, rows(0), 0:LANES] if step else 0.0 for j in range(4)]
+            for n in (2 * step, 2 * step + 1):
+                lanes = slice(n * LANES, (n + 1) * LANES)
+                t = source_ref[rows(0), lanes]
+                u = [source_ref[rows(1 + x), lanes] for x in range(3)]
+                paths = [radial_ref[0, rows(j), lanes] for j in range(4)]
+                r = [r_ref[x, n] for x in range(3)]
+                along = r[0] * u[0] + r[1] * u[1] + r[2] * u[2]
+                sums[0] = sums[0] + (paths[0] * t + paths[1] * along)
+                turned = paths[2] * t
+                for x in range(3):
+                    sums[1 + x] = sums[1 + x] + (turned * r[x] + paths[3] * u[x])
+            for j in range(4):
+                node_ref[j, rows(0), 0:LANES] = sums[j]
+
+    for step in range(own_edges // 256):
+        edge_step(step, 0)
+        if step:
+            sum_slots(step - 1)
+    sum_slots(own_edges // 256 - 1)
+
+
+    ready("pulls")
 
     scalar_two = node_ref[0, :, 0:LANES]
     vector_two = [node_ref[1 + x, :, 0:LANES] for x in range(3)]
@@ -503,7 +510,7 @@
         mixes_ref[1], jnp.concatenate([data_stack(scalar_two), data_stack(squares_two)], axis=0)
     )
     gate_two = sigmoid(before_two)
-    readout = readout_ref[...]
+    readout = sum(turns_ref[6, :, i * LANES : (i + 1) * LANES].astype(F32) for i in (1, 2))
     energy_ref[0, 0] = jnp.sum(readout * (before_two * gate_two), axis=0, keepdims=True)
     dbefore_two = readout * (gate_two * (1.0 + before_two * (1.0 - gate_two)))
     dbefore_two = data_stack(dbefore_two)
@@ -513,11 +520,11 @@
     for x in range(3):
         node_ref[1 + x, :, 0:LANES] = 2.0 * vector_two[x] * dsquares_two
 
-    def back_step(n, carry):
-        lanes = pl.ds(pl.multiple_of(n * LANES, LANES), LANES)
+    def back_slot(n, half):
+        lanes = slice(n * LANES, (n + 1) * LANES)
         r = [jnp.concatenate([r_ref[x, n]] * 2, axis=0) for x in range(3)]
         totals = [jnp.zeros((16, LANES), F32) for _ in range(4)]
-        for part in range(channels // 16):
+        for part in range(half * channels // 32, (half + 1) * channels // 32):
 
             def rows(j):
                 return slice(j * channels + part * 16, j * channels + part * 16 + 16)
@@ -544,16 +551,23 @@
                 dsource_ref[0, rows(j), lanes], dsource_ref[1, rows(j), lanes] = split(dsource[j])
         dd = 2.0 * jnp.sum(totals[3], axis=0, keepdims=True)
         for x in range(3):
-            total = jnp.sum(totals[x], axis=0, keepdims=True)
-            dr_ref[x : x + 1, lanes] = total + dd * r_ref[x, n, 0:1, :]
-        return carry
-
-    lax.fori_loop(0, 16, back_step, 0)
-
-    source_ref[:, 0:atoms] = dot_nt(dsource_ref[0], pair_ref[0:atoms, :]) + dot_nt(
-        dsource_ref[1], pair_ref[0:atoms, :]
-    )
-    dfeat = source_ref[:, 0:atoms]
+            total = jnp.sum(totals[x], axis=0, keepdims=True) + dd * r_ref[x, n, 0:1, :]
+            if half:
+                total = total + dr_ref[x : x + 1, lanes]
+            dr_ref[x : x + 1, lanes] = total
+
+    for half in range(2):
+        for n in range(16):
+            back_slot(n, half)
+        size = channels // 2
+        picked = [slice(j * channels + half * size, j * channels + half * size + size) for j in range(4)]
+        stack = [dsource_ref[i, at, :] for i in range(2) for at in picked]
+        spread = dot_nt(jnp.concatenate(stack, axis=0), pair_ref[0:atoms, :])
+        for j in range(4):
+            high = spread[j * size : (j + 1) * size]
+            dfeat_ref[picked[j], :] = high + spread[(4 + j) * size : (5 + j) * size]
+
+    dfeat = dfeat_ref[...]
     gain_one = node_ref[4, :, 0:atoms]
     vector_one = [node_ref[5 + x, :, 0:atoms] for x in range(3)]
     dbefore_one = data_stack(dfeat[0:channels] * gain_one)
@@ -722,21 +736,19 @@
         functools.partial(prepare_kernel, dims),
         out_shape=(
             jax.ShapeDtypeStruct((atoms, edges), BF16),
-            jax.ShapeDtypeStruct((2, 4 * radial_in.shape[0], 2 * hidden), BF16),
             jax.ShapeDtypeStruct((2, channels, 3 * kinds * hidden), BF16),
             jax.ShapeDtypeStruct((2, kinds * hidden, 3 * channels), BF16),
             jax.ShapeDtypeStruct((2, channels, 6 * channels), BF16),
-            jax.ShapeDtypeStruct((6, channels, 3 * channels), BF16),
+            jax.ShapeDtypeStruct((7, channels, 3 * channels), BF16),
             jax.ShapeDtypeStruct((4 * channels, 3 * hidden), BF16),
-            jax.ShapeDtypeStruct((channels, LANES), F32),
         ),
         in_specs=[vmem] * 12,
-        out_specs=(vmem,) * 8,
+        out_specs=(vmem,) * 6,
         compiler_params=pltpu.CompilerParams(vmem_limit_bytes=VMEM_BYTES),
         cost_estimate=pl.CostEstimate(flops=0, bytes_accessed=8 * 1024 * 1024, transcendentals=0),
     )(neighbours, *weights)
     grads, energy = pl.pallas_call(
-        functools.partial(main_kernel, dims, near, whole),
+        functools.partial(main_kernel, dims, near, whole, radial_in.shape[0]),
         out_shape=(
             jax.ShapeDtypeStruct((windows, 8, LANES), F32),
             jax.ShapeDtypeStruct((1, 1, 1, LANES), F32),
@@ -762,8 +774,12 @@
             pltpu.VMEM((2 * atoms, edges), BF16),
         ]
         + [pltpu.VMEM(p.shape, p.dtype) for p in prepared[1:]]
-        + [pltpu.SemaphoreType.DMA((len(prepared) + 1,))],
-        compiler_params=pltpu.CompilerParams(vmem_limit_bytes=VMEM_BYTES),
+        + [
+            pltpu.SemaphoreType.DMA((len(prepared) + 1,)),
+            pltpu.VMEM((groups - 1, 16, LANES), jnp.int32),
+            pltpu.VMEM((4 * channels, atoms), F32),
+        ],
+        compiler_params=pltpu.CompilerParams(vmem_limit_bytes=MAIN_BYTES),
     )(table, neighbours, *prepared)
 
     if whole:

time: 56.8 us -> 50.6 us (0.89)
  Pallas kernels: 33.3 us -> 28.1 us
  blocking collectives: 11 us -> 10.2 us
    pallas_call x1, Pallas kernels: 26.8 us -> 21.4 us  [per_device(): pl.pallas_call(functools.partial(main_kernel, dims, near, whole, radial_i...]
    all_to_all x1, blocking collectives: 11 us -> 10.2 us  [per_device(): returned = lax.all_to_all(grads, AXES, 0, 0, tiled=True)]
  transfers between devices with their start and end apart: 1 -> 1, of which waited for: 1 -> 1; matrix products, arithmetic and copies ran while one was open for 0% -> 0% of each run, Pallas kernels for 6% -> 7%
where the time goes in v2:
time: 50.6 us; the launch traced here: 50.2 us
  Pallas kernels  28.1 us (56%)
  blocking collectives  10.2 us (20%)
  starting transfers between devices  7.36 us (15%)
  waiting for transfers between devices  3.22 us (6%)
  local copies, waits for them, and re-layouts  0.7 us (1%)
  between operations  0.65 us (1%)
    pallas_call x1, Pallas kernels, per_device(): pl.pallas_call(functools.partial(main_kernel, dims, near, whole, radial_i...  21.4 us
    all_to_all x1, blocking collectives, per_device(): returned = lax.all_to_all(grads, AXES, 0, 0, tiled=True)  10.2 us
    all_to_all x1, starting transfers between devices, per_device(): table = lax.all_to_all(packed, AXES, 0, 0, tiled=True)  7.36 us
    pallas_call x1, Pallas kernels, per_device(): pl.pallas_call(functools.partial(prepare_kernel, dims), out_shape=(jax.Sh...  3.68 us
    all_to_all x1, waiting for transfers between devices, per_device(): table = lax.all_to_all(packed, AXES, 0, 0, tiled=True)  3.22 us
    pallas_call x1, Pallas kernels, per_device(): pl.pallas_call(functools.partial(pack_kernel, copies), out_shape=jax.Shap...  1.52 us
    pallas_call x1, Pallas kernels, per_device(): pl.pallas_call(functools.partial(forces_kernel, copies), out_shape=jax.Sh...  1.5 us
  transfers between devices with their start and end apart: 1, of which 1 were waited for; matrix products, arithmetic and copies ran while one was open for 0% of the time, Pallas kernels for 7%

profile of v2, /device:TPU:0, one launch (start us, length us, event | category | flops | bytes accessed | tf_op | source)
XLA Modules:
  0.0 50.2 jit_solution(3744059149364726285)
XLA Ops:
  0.6 1.5 %shard_map.158 = f32[16,8,128]{2,1,0:T(8,128)} custom-call(s32[1,1,1,16]{3,2,1,0:T(1,128)} %send_ref.3, f32[3,1,1,1,128]{4,3,2,1,0:T(1,128)} %pos_ref.1, s32[1,1,1,128]{3,2,1,0:T(1,128)} %species_ref.1, s32[1,1,1,16,128]{4,3,2,1,0:T(8,128)} %neigh_ref.5), custom_call_target="tpu_custom_call" | custom-call | tf_op jit(solution)/shard_map/pallas_call | solution.py:702
  2.1 7.4 %all-to-all-start = ((f32[16,8,128]{2,1,0:T(8,128)}), f32[16,8,128]{2,1,0:T(8,128)S(1)}, u32[]{:S(2)}, u32[]{:S(2)}) async-start(f32[16,8,128]{2,1,0:T(8,128)} %shard_map.158), calls=%async_computation | async-start | bytes 131072 | tf_op jit(solution)/shard_map/all_to_all | solution.py:710
  9.5 3.7 %shard_map.159 = (bf16[384,2048]{1,0:T(8,128)(2,1)}, bf16[2,128,960]{2,1,0:T(8,128)(2,1)}, bf16[2,320,384]{2,1,0:T(8,128)(2,1)}, bf16[2,128,768]{2,1,0:T(8,128)(...) custom-call(s32[1,1,1,16,128]{4,3,2,1,0:T(8,128)} %neigh_ref.5, f32[5,128]{1,0:T(8,128)} %embedding_ref.1, ...), custom_call_target="tpu_custom_call" | custom-call | bytes 8388608 | tf_op jit(solution)/shard_map/pallas_call | solution.py:735
  13.2 3.2 %all-to-all-done.table_ref = f32[16,8,128]{2,1,0:T(8,128)S(1)} async-done(((f32[16,8,128]{2,1,0:T(8,128)}), f32[16,8,128]{2,1,0:T(8,128)S(1)}, u32[]{:S(2)}, u32[]{:S(2)}) %all-to-all-start) | async-done | bytes 65568 | tf_op jit(solution)/shard_map/all_to_all | solution.py:710
  16.4 0.0 copy-start
  16.4 0.7 %copy-done = s32[1,1,1,16,128]{4,3,2,1,0:T(8,128)S(1)} copy-done((s32[1,1,1,16,128]{4,3,2,1,0:T(8,128)S(1)}, s32[1,1,1,16,128]{4,3,2,1,0:T(8,128)}, u32[]{:S(2)}) %copy-start) | copy-done | bytes 8216
  17.1 21.4 %shard_map.160 = (f32[16,8,128]{2,1,0:T(8,128)S(1)}, f32[1,1,1,128]{3,2,1,0:T(1,128)}) custom-call(f32[16,8,128]{2,1,0:T(8,128)S(1)} %all-to-all-done.table_ref, s32[1,1,1,16,128]{4,3,2,1,0:T(8,128)S(1)} %copy-done, bf16[384,2048]{1,0:T(8,128)(2,1)} %get-tuple-element.10.pair_hbm, bf16[2,128,960]{2,1,0:T(8,128)(2,1)} %get-tuple-element.11.slots_hbm, ...), custom_call_target="tpu_custom_call" | custom-call | tf_op jit(solution)/shard_map/pallas_call | solution.py:750
  38.5 10.2 %all_to_all.10.parts_ref = f32[16,8,128]{2,1,0:T(8,128)} all-to-all(f32[16,8,128]{2,1,0:T(8,128)S(1)} %get-tuple-element.16), channel_id=1, replica_groups=mesh['groups'=2,'gx'=4,'gy'=2,'gz'=2] {'gx','gy','gz'}, dimensions={0} | all-to-all | bytes 131072 | tf_op jit(solution)/shard_map/all_to_all | solution.py:786
  48.7 1.5 %shard_map.161 = f32[3,1,1,1,128]{4,3,2,1,0:T(1,128)} custom-call(s32[1,1,1,16]{3,2,1,0:T(1,128)} %send_ref.3, f32[16,8,128]{2,1,0:T(8,128)} %all_to_all.10.parts_ref), custom_call_target="tpu_custom_call" | custom-call | tf_op jit(solution)/shard_map/pallas_call | solution.py:798
Async XLA Ops:
  2.1 14.3 %all-to-all-start = ((f32[16,8,128]{2,1,0:T(8,128)}), f32[16,8,128]{2,1,0:T(8,128)S(1)}, u32[]{:S(2)}, u32[]{:S(2)}) async-start(f32[16,8,128]{2,1,0:T(8,128)} %shard_map.158), calls=%async_computation | async-start | bytes 131072 | tf_op jit(solution)/shard_map/all_to_all | solution.py:710
  16.4 0.7 %copy-start = (s32[1,1,1,16,128]{4,3,2,1,0:T(8,128)S(1)}, s32[1,1,1,16,128]{4,3,2,1,0:T(8,128)}, u32[]{:S(2)}) copy-start(s32[1,1,1,16,128]{4,3,2,1,0:T(8,128)} %neigh_ref.5) | copy-start | bytes 24580

commit v3 on v2

--- a/solution.py
+++ b/solution.py
@@ -218,7 +218,10 @@
     paths_ref[...] = jnp.transpose(jnp.concatenate([high, low, high], axis=0)).astype(BF16)
     read = jnp.transpose(jnp.broadcast_to(readout_ref[...], (LANES, channels)))
     turns_ref[6, :, LANES : 2 * LANES], turns_ref[6, :, 2 * LANES : 3 * LANES] = split(read)
-    turns_ref[6, 8 * basis : channels, 0:LANES] = jnp.zeros((channels - 8 * basis, LANES), BF16)
+    lists = jnp.concatenate(split(entries.astype(F32)), axis=0)
+    turns_ref[6, 8 * basis : 8 * basis + 32, 0:LANES] = lists
+    rest = channels - 8 * basis - 32
+    turns_ref[6, channels - rest : channels, 0:LANES] = jnp.zeros((rest, LANES), BF16)
 
 
 def main_kernel(
@@ -227,7 +230,6 @@
     whole,
     rank,
     table_ref,
-    neigh_ref,
     pair_hbm,
     slots_hbm,
     pulls_hbm,
@@ -312,10 +314,12 @@
         picked = jnp.take_along_axis(block, index, axis=1)
         sent[w // 8] = jnp.where((lane8 >> 4) == w % 8, picked, sent[w // 8])
 
-    for g in range(groups):
+    for g in [*range(1, groups), 0]:
         members = [] if g == 0 else list(range((g - 1) * 8, min(g * 8, len(near))))
         if g == 0:
-            entries = neigh_ref[0, 0, 0]
+            ready("turns")
+            lists = turns_ref[6, 8 * rank : 8 * rank + 32, 0:LANES].astype(F32)
+            entries = (lists[0:16] + lists[16:32]).astype(jnp.int32)
             own_block = table_ref[own_place]
             centre = [own_block[x : x + 1] for x in range(3)]
             steps = [0, 0, 0]
@@ -374,8 +378,6 @@
         row = jnp.where(local, local_index, LANES + sent_index)
         place_ref[g - 1] = jnp.where(valid, row, -1)
 
-    ready("turns")
-
     rates = decay_rates(basis)
 
     def radial_rows(weights, octet):
@@ -753,7 +755,7 @@
             jax.ShapeDtypeStruct((windows, 8, LANES), F32),
             jax.ShapeDtypeStruct((1, 1, 1, LANES), F32),
         ),
-        in_specs=[vmem] * 2 + [pl.BlockSpec(memory_space=pltpu.HBM)] * len(prepared),
+        in_specs=[vmem] + [pl.BlockSpec(memory_space=pltpu.HBM)] * len(prepared),
         out_specs=(vmem, vmem),
         scratch_shapes=[
             pltpu.VMEM((3, rows, 8, LANES), F32),
@@ -780,7 +782,7 @@
             pltpu.VMEM((4 * channels, atoms), F32),
         ],
         compiler_params=pltpu.CompilerParams(vmem_limit_bytes=MAIN_BYTES),
-    )(table, neighbours, *prepared)
+    )(table, *prepared)
 
     if whole:
         returned = lax.all_to_all(grads, AXES, 0, 0, tiled=True)

time: 50.6 us -> 49.9 us (0.986)
  local copies, waits for them, and re-layouts: 0.7 us -> 0 us
    unnamed x2 -> x0, local copies, waits for them, and re-layouts: 0.7 us -> none
where the time goes in v3:
time: 49.9 us; the launch traced here: 49.6 us
  Pallas kernels  28.2 us (57%)
  blocking collectives  10.2 us (20%)
  starting transfers between devices  7.36 us (15%)
  waiting for transfers between devices  3.23 us (6%)
  between operations  0.65 us (1%)
    pallas_call x1, Pallas kernels, per_device(): pl.pallas_call(functools.partial(main_kernel, dims, near, whole, radial_i...  21.5 us
    all_to_all x1, blocking collectives, per_device(): returned = lax.all_to_all(grads, AXES, 0, 0, tiled=True)  10.2 us
    all_to_all x1, starting transfers between devices, per_device(): table = lax.all_to_all(packed, AXES, 0, 0, tiled=True)  7.36 us
    pallas_call x1, Pallas kernels, per_device(): pl.pallas_call(functools.partial(prepare_kernel, dims), out_shape=(jax.Sh...  3.67 us
    all_to_all x1, waiting for transfers between devices, per_device(): table = lax.all_to_all(packed, AXES, 0, 0, tiled=True)  3.23 us
    pallas_call x1, Pallas kernels, per_device(): pl.pallas_call(functools.partial(pack_kernel, copies), out_shape=jax.Shap...  1.52 us
    pallas_call x1, Pallas kernels, per_device(): pl.pallas_call(functools.partial(forces_kernel, copies), out_shape=jax.Sh...  1.5 us
  transfers between devices with their start and end apart: 1, of which 1 were waited for; matrix products, arithmetic and copies ran while one was open for 0% of the time, Pallas kernels for 7%

profile of v3, /device:TPU:0, one launch (start us, length us, event | category | flops | bytes accessed | tf_op | source)
XLA Modules:
  0.0 49.6 jit_solution(9606079570251975982)
XLA Ops:
  0.6 1.5 %shard_map.158 = f32[16,8,128]{2,1,0:T(8,128)} custom-call(s32[1,1,1,16]{3,2,1,0:T(1,128)} %send_ref.3, f32[3,1,1,1,128]{4,3,2,1,0:T(1,128)} %pos_ref.1, s32[1,1,1,128]{3,2,1,0:T(1,128)} %species_ref.1, s32[1,1,1,16,128]{4,3,2,1,0:T(8,128)} %neigh_ref.3), custom_call_target="tpu_custom_call" | custom-call | tf_op jit(solution)/shard_map/pallas_call | solution.py:704
  2.1 7.4 %all-to-all-start = ((f32[16,8,128]{2,1,0:T(8,128)}), f32[16,8,128]{2,1,0:T(8,128)S(1)}, u32[]{:S(2)}, u32[]{:S(2)}) async-start(f32[16,8,128]{2,1,0:T(8,128)} %shard_map.158), calls=%async_computation | async-start | bytes 131072 | tf_op jit(solution)/shard_map/all_to_all | solution.py:712
  9.5 3.7 %shard_map.159 = (bf16[384,2048]{1,0:T(8,128)(2,1)}, bf16[2,128,960]{2,1,0:T(8,128)(2,1)}, bf16[2,320,384]{2,1,0:T(8,128)(2,1)}, bf16[2,128,768]{2,1,0:T(8,128)(...) custom-call(s32[1,1,1,16,128]{4,3,2,1,0:T(8,128)} %neigh_ref.3, f32[5,128]{1,0:T(8,128)} %embedding_ref.1, ...), custom_call_target="tpu_custom_call" | custom-call | bytes 8388608 | tf_op jit(solution)/shard_map/pallas_call | solution.py:737
  13.2 3.2 %all-to-all-done.table_ref = f32[16,8,128]{2,1,0:T(8,128)S(1)} async-done(((f32[16,8,128]{2,1,0:T(8,128)}), f32[16,8,128]{2,1,0:T(8,128)S(1)}, u32[]{:S(2)}, u32[]{:S(2)}) %all-to-all-start) | async-done | bytes 65568 | tf_op jit(solution)/shard_map/all_to_all | solution.py:712
  16.4 21.5 %shard_map.160 = (f32[16,8,128]{2,1,0:T(8,128)S(1)}, f32[1,1,1,128]{3,2,1,0:T(1,128)}) custom-call(f32[16,8,128]{2,1,0:T(8,128)S(1)} %all-to-all-done.table_ref, bf16[384,2048]{1,0:T(8,128)(2,1)} %get-tuple-element.10.pair_hbm, bf16[2,128,960]{2,1,0:T(8,128)(2,1)} %get-tuple-element.11.slots_hbm, bf16[2,320,384]{2,1,0:T(8,128)(2,1)} %get-tuple-element.12.pulls_hbm, ...), custom_call_target="tpu_custom_call" | custom-call | tf_op jit(solution)/shard_map/pallas_call | solution.py:752
  37.9 10.2 %all_to_all.10.parts_ref = f32[16,8,128]{2,1,0:T(8,128)} all-to-all(f32[16,8,128]{2,1,0:T(8,128)S(1)} %get-tuple-element.16), channel_id=1, replica_groups=mesh['groups'=2,'gx'=4,'gy'=2,'gz'=2] {'gx','gy','gz'}, dimensions={0} | all-to-all | bytes 131072 | tf_op jit(solution)/shard_map/all_to_all | solution.py:788
  48.1 1.5 %shard_map.161 = f32[3,1,1,1,128]{4,3,2,1,0:T(1,128)} custom-call(s32[1,1,1,16]{3,2,1,0:T(1,128)} %send_ref.3, f32[16,8,128]{2,1,0:T(8,128)} %all_to_all.10.parts_ref), custom_call_target="tpu_custom_call" | custom-call | tf_op jit(solution)/shard_map/pallas_call | solution.py:800
Async XLA Ops:
  2.1 14.3 %all-to-all-start = ((f32[16,8,128]{2,1,0:T(8,128)}), f32[16,8,128]{2,1,0:T(8,128)S(1)}, u32[]{:S(2)}, u32[]{:S(2)}) async-start(f32[16,8,128]{2,1,0:T(8,128)} %shard_map.158), calls=%async_computation | async-start | bytes 131072 | tf_op jit(solution)/shard_map/all_to_all | solution.py:712

commit v4 on v3

--- a/solution.py
+++ b/solution.py
@@ -425,14 +425,17 @@
         for n in range(16):
             e = g * 16 + n
             kind = kind_ref[e]
-            masks = [kind == float(s) for s in range(kinds)]
+            masks = [kind == float(s) for s in range(kinds - 1)]
             for i in range(2):
                 value = wh_ref[e, pl.ds(pl.multiple_of(part * 16 + i * 8, 8), 8), :]
                 parts = [value] + [value * r_ref[x, e] for x in range(3)]
-                for s in range(kinds):
-                    for j in range(4):
+                for j in range(4):
+                    sums[i][-1][j] = sums[i][-1][j] + parts[j]
+                    for s in range(kinds - 1):
                         sums[i][s][j] = sums[i][s][j] + jnp.where(masks[s], parts[j], 0.0)
         for i in range(2):
+            for j in range(4):
+                sums[i][-1][j] = sums[i][-1][j] - sum(sums[i][s][j] for s in range(kinds - 1))
             for s in range(kinds):
                 place = pl.ds(pl.multiple_of(s * hidden + part * 16 + i * 8, 8), 8)
                 for j in range(4):

time: 49.9 us -> 49.6 us (level)
  no operation moved by 1% of the time
where the time goes in v4:
time: 49.6 us; the launch traced here: 49.2 us
  Pallas kernels  27.8 us (56%)
  blocking collectives  10.2 us (21%)
  starting transfers between devices  7.36 us (15%)
  waiting for transfers between devices  3.23 us (7%)
  between operations  0.65 us (1%)
    pallas_call x1, Pallas kernels, per_device(): pl.pallas_call(functools.partial(main_kernel, dims, near, whole, radial_i...  21.1 us
    all_to_all x1, blocking collectives, per_device(): returned = lax.all_to_all(grads, AXES, 0, 0, tiled=True)  10.2 us
    all_to_all x1, starting transfers between devices, per_device(): table = lax.all_to_all(packed, AXES, 0, 0, tiled=True)  7.36 us
    pallas_call x1, Pallas kernels, per_device(): pl.pallas_call(functools.partial(prepare_kernel, dims), out_shape=(jax.Sh...  3.67 us
    all_to_all x1, waiting for transfers between devices, per_device(): table = lax.all_to_all(packed, AXES, 0, 0, tiled=True)  3.23 us
    pallas_call x1, Pallas kernels, per_device(): pl.pallas_call(functools.partial(pack_kernel, copies), out_shape=jax.Shap...  1.52 us
    pallas_call x1, Pallas kernels, per_device(): pl.pallas_call(functools.partial(forces_kernel, copies), out_shape=jax.Sh...  1.5 us
  transfers between devices with their start and end apart: 1, of which 1 were waited for; matrix products, arithmetic and copies ran while one was open for 0% of the time, Pallas kernels for 7%

profile of v4, /device:TPU:0, one launch (start us, length us, event | category | flops | bytes accessed | tf_op | source)
XLA Modules:
  0.0 49.2 jit_solution(4385690682389354148)
XLA Ops:
  0.6 1.5 %shard_map.158 = f32[16,8,128]{2,1,0:T(8,128)} custom-call(s32[1,1,1,16]{3,2,1,0:T(1,128)} %send_ref.3, f32[3,1,1,1,128]{4,3,2,1,0:T(1,128)} %pos_ref.1, s32[1,1,1,128]{3,2,1,0:T(1,128)} %species_ref.1, s32[1,1,1,16,128]{4,3,2,1,0:T(8,128)} %neigh_ref.3), custom_call_target="tpu_custom_call" | custom-call | tf_op jit(solution)/shard_map/pallas_call | solution.py:707
  2.1 7.4 %all-to-all-start = ((f32[16,8,128]{2,1,0:T(8,128)}), f32[16,8,128]{2,1,0:T(8,128)S(1)}, u32[]{:S(2)}, u32[]{:S(2)}) async-start(f32[16,8,128]{2,1,0:T(8,128)} %shard_map.158), calls=%async_computation | async-start | bytes 131072 | tf_op jit(solution)/shard_map/all_to_all | solution.py:715
  9.5 3.7 %shard_map.159 = (bf16[384,2048]{1,0:T(8,128)(2,1)}, bf16[2,128,960]{2,1,0:T(8,128)(2,1)}, bf16[2,320,384]{2,1,0:T(8,128)(2,1)}, bf16[2,128,768]{2,1,0:T(8,128)(...) custom-call(s32[1,1,1,16,128]{4,3,2,1,0:T(8,128)} %neigh_ref.3, f32[5,128]{1,0:T(8,128)} %embedding_ref.1, ...), custom_call_target="tpu_custom_call" | custom-call | bytes 8388608 | tf_op jit(solution)/shard_map/pallas_call | solution.py:740
  13.2 3.2 %all-to-all-done.table_ref = f32[16,8,128]{2,1,0:T(8,128)S(1)} async-done(((f32[16,8,128]{2,1,0:T(8,128)}), f32[16,8,128]{2,1,0:T(8,128)S(1)}, u32[]{:S(2)}, u32[]{:S(2)}) %all-to-all-start) | async-done | bytes 65568 | tf_op jit(solution)/shard_map/all_to_all | solution.py:715
  16.4 21.1 %shard_map.160 = (f32[16,8,128]{2,1,0:T(8,128)S(1)}, f32[1,1,1,128]{3,2,1,0:T(1,128)}) custom-call(f32[16,8,128]{2,1,0:T(8,128)S(1)} %all-to-all-done.table_ref, bf16[384,2048]{1,0:T(8,128)(2,1)} %get-tuple-element.10.pair_hbm, bf16[2,128,960]{2,1,0:T(8,128)(2,1)} %get-tuple-element.11.slots_hbm, bf16[2,320,384]{2,1,0:T(8,128)(2,1)} %get-tuple-element.12.pulls_hbm, ...), custom_call_target="tpu_custom_call" | custom-call | tf_op jit(solution)/shard_map/pallas_call | solution.py:755
  37.6 10.2 %all_to_all.10.parts_ref = f32[16,8,128]{2,1,0:T(8,128)} all-to-all(f32[16,8,128]{2,1,0:T(8,128)S(1)} %get-tuple-element.16), channel_id=1, replica_groups=mesh['groups'=2,'gx'=4,'gy'=2,'gz'=2] {'gx','gy','gz'}, dimensions={0} | all-to-all | bytes 131072 | tf_op jit(solution)/shard_map/all_to_all | solution.py:791
  47.7 1.5 %shard_map.161 = f32[3,1,1,1,128]{4,3,2,1,0:T(1,128)} custom-call(s32[1,1,1,16]{3,2,1,0:T(1,128)} %send_ref.3, f32[16,8,128]{2,1,0:T(8,128)} %all_to_all.10.parts_ref), custom_call_target="tpu_custom_call" | custom-call | tf_op jit(solution)/shard_map/pallas_call | solution.py:803
Async XLA Ops:
  2.1 14.3 %all-to-all-start = ((f32[16,8,128]{2,1,0:T(8,128)}), f32[16,8,128]{2,1,0:T(8,128)S(1)}, u32[]{:S(2)}, u32[]{:S(2)}) async-start(f32[16,8,128]{2,1,0:T(8,128)} %shard_map.158), calls=%async_computation | async-start | bytes 131072 | tf_op jit(solution)/shard_map/all_to_all | solution.py:715
